TPU v7x, 128 devices: a whole 4x4x4 slice. The times are simulated.
128 devices in a mesh: row: 4 (over x), col: 32 (over z, y, core).
Axes of the slice: x: 4, y: 4, z: 4, core: 2. Of those that a mesh axis runs over, the one named last changes fastest.
Arguments:
- stiffness: bfloat16 [160, 1024, 1024], P('col', 'row'), may hold values from -0.1875 to 0.1875
- coupling: bfloat16 [160, 1024, 2, 768], P('col', 'row'), may hold values from -1.0546875 to 1.0546875
- slave_diag: float32 [160, 1024], P('col', 'row'), may hold values from 0.5 to 2
- slave_masters: int32 [160, 2], P('col'), may hold values from 0 to 31, all different within a row; in each aligned block of 5 rows (0 to 4, 5 to 9, ...) at most 2 rows name the same one
Outputs:
- cross_fill: bfloat16 [160, 768, 768], P('col', 'row')
- diag_fill: bfloat16 [32, 768, 768], P('col', 'row')
Inputs may be any that keep to these rules, and one draw needn't show every extreme that they name: `slave_masters`: each slave block names two different master blocks; among the slave blocks of one index of col no master block is named more than 2 times, and some master block is named exactly 2 times; every master block is named somewhere.
All inputs are finite; a program needn't handle non-finite values.
Results may differ from a plain program's by a relative error of at most 0.0071.
Values may be sent and summed in bfloat16 or wider, within the bound.
A program may use at most 192 MiB of HBM per device.

v0:
```python
import jax
import jax.numpy as jnp
from jax import lax
from jax.sharding import PartitionSpec as P


def pair_fills(first, second, applied, width):
    right_first = applied[:, :, :width]
    right_second = applied[:, :, width:]
    fill_aa = jnp.einsum("snr,snc->rsc", first, right_first, preferred_element_type=jnp.float32)
    fill_bb = jnp.einsum("snr,snc->rsc", second, right_second, preferred_element_type=jnp.float32)
    fill_ab = jnp.einsum("snr,snc->rsc", first, right_second, preferred_element_type=jnp.float32)
    return jnp.stack((fill_aa, fill_bb, fill_ab), axis=2)


def per_device(stiffness, coupling, slave_diag, slave_masters):
    blocks, local_rows, total_rows = stiffness.shape
    width = coupling.shape[-1]
    row_count = lax.axis_size("row")
    col_count = lax.axis_size("col")
    share = width // row_count
    projected = (coupling.astype(jnp.float32) / slave_diag[:, :, None, None]).astype(jnp.bfloat16)
    projected = projected.reshape(blocks, local_rows, 2 * width)
    applied = jnp.einsum(
        "srk,skc->src",
        stiffness,
        lax.all_gather(projected, "row", axis=1, tiled=True),
        preferred_element_type=jnp.float32,
    ).astype(jnp.bfloat16)
    left_first = lax.slice_in_dim(projected, 0, share * lax.axis_size("row"), axis=2)
    left_second = lax.dynamic_slice_in_dim(projected, width, share * lax.axis_size("row"), 2)
    fills = lax.psum_scatter(
        pair_fills(left_first, left_second, applied, width), "row", scatter_dimension=0, tiled=True
    )
    rounded = fills.astype(jnp.bfloat16)
    cross_fill = jnp.transpose(rounded[:, :, 2], (1, 0, 2))
    terms = rounded[:, :, :2].reshape(share, blocks * 2, width)
    targets = slave_masters.reshape(blocks * 2)
    owners_all = jnp.arange(col_count)
    onehot = (targets[:, None] == owners_all[None, :]).astype(jnp.bfloat16)
    outgoing = jnp.einsum("rec,ep->prc", terms, onehot, preferred_element_type=jnp.float32).astype(
        jnp.bfloat16
    )
    incoming = lax.all_to_all(outgoing, "col", split_axis=0, concat_axis=0, tiled=True)
    diag_fill = jnp.sum(incoming, axis=0, dtype=jnp.float32).astype(jnp.bfloat16)[None]
    return (cross_fill, diag_fill)


def solution(mesh):
    return jax.shard_map(
        per_device,
        mesh=mesh,
        in_specs=(
            P("col", "row", None),
            P("col", "row", None, None),
            P("col", "row"),
            P("col", None),
        ),
        out_specs=(P("col", "row", None), P("col", "row", None)),
        check_vma=False,
    )
```

profile of v0, /device:TPU:1, one launch (start us, length us, event | category | flops | bytes accessed | tf_op | source)
XLA Modules:
  0.0 780.3 jit_solution(4377785647032288502)
XLA Ops:
  7.2 0.0 copy-start
  7.2 0.0 all-gather.2.cloned.1.call-start
  7.2 8.6 %fusion = bf16[5,256,2,768]{3,2,1,0:T(2,128)(2,1)} fusion(bf16[5,256,2,768]{3,2,1,0:T(2,128)(2,1)} %param.5, f32[5,256]{1,0:T(8,128)} %param.6), kind=kLoop, calls=%fused_computation.3 | loop fusion | flops 5898240 | bytes 7869440 | tf_op jit(solution)/shard_map/convert_element_type | solution.py:22
  15.8 10.4 %copy.20 = bf16[5,256,2,768]{1,3,2,0:T(8,128)(2,1)} copy(bf16[5,256,2,768]{3,2,1,0:T(2,128)(2,1)} %fusion) | data formatting | bytes 7864320 | tf_op jit(solution)/shard_map/convert_element_type | solution.py:22
  26.2 0.0 all-gather.2.cloned.1.call-update
  26.3 0.0 reduce-scatter.4.cloned.1.call-start
  26.3 151.9 %all-gather.2.cloned.1.call-done = bf16[5,1024,1536]{1,2,0:T(8,128)(2,1)} async-done(((bf16[5,256,1536]{1,2,0:T(8,128)(2,1)}), bf16[5,1024,1536]{1,2,0:T(8,128)(2,1)}) %all-gather.2.cloned.1.call-update) | async-done | bytes 15728656 | tf_op jit(solution)/shard_map/all_gather | solution.py:27
  178.2 0.0 copy-done
  178.2 11.7 %fusion.2 = bf16[5,256,1536]{1,2,0:T(8,128)(2,1)} fusion(bf16[5,1024,1536]{1,2,0:T(8,128)(2,1)} %all-gather.2.cloned.1.call-done, bf16[5,256,1024]{2,1,0:T(8,128)(2,1)S(1)} %copy-done), kind=kOutput, calls=%fused_computation.10 | convolution fusion | flops 4028497920 | bytes 22282240 | tf_op jit(solution)/shard_map/srk,skc->src/dot_general | solution.py:24
  189.9 4.0 convolution_bitcast_fusion.1
  194.0 0.0 copy-done.2
  194.0 3.3 convolution_bitcast_fusion.2
  197.3 7.7 convolution_bitcast_fusion
  204.9 17.0 %pad_maximum_fusion = f32[768,5,3,768]{0,3,1,2:T(8,128)} fusion(f32[768,5,1,768]{0,3,1,2:T(8,128)} %convolution_bitcast_fusion, f32[768,5,1,768]{0,3,1,2:T(8,128)S(1)} %convolution_bitcast_fusion.1, f32[768,5,1,768]{0,3,1,2:T(8,128)S(1)} %convolution_bitcast_fusion.2), kind=kLoop, calls=%fused_computation | loop fusion | flops 17694720 | bytes 70778880 | tf_op jit(solution)/shard_map/stack | solution.py:13
  222.0 47.2 %copy.31 = f32[768,5,3,768]{3,1,2,0:T(8,128)} copy(f32[768,5,3,768]{0,3,1,2:T(8,128)} %pad_maximum_fusion) | data formatting | bytes 70778880
  269.2 44.3 %reshape.15 = f32[768,11520]{1,0:T(8,128)} reshape(f32[768,3,5,768]{3,2,1,0:T(8,128)} %bitcast.29) | data formatting | bytes 70778880
  313.6 0.0 reduce-scatter.4.cloned.1.call-update
  313.6 0.7 copy-done.4
  314.2 0.1 copy.25
  314.3 0.1 eq.15
  314.4 298.1 %reduce-scatter.4.cloned.1.call-done = f32[192,11520]{1,0:T(8,128)} async-done(((f32[768,11520]{1,0:T(8,128)}), f32[192,11520]{1,0:T(8,128)}) %reduce-scatter.4.cloned.1.call-update) | async-done | bytes 8847376
  612.5 10.2 %reshape.16 = bf16[192,3,5,768]{3,2,1,0:T(8,128)(2,1)} reshape(f32[192,11520]{1,0:T(8,128)} %reduce-scatter.4.cloned.1.call-done) | data formatting | bytes 13271040
  622.7 4.1 copy.37
  626.7 2.1 copy-done.3
  628.8 0.2 slice.24
  629.1 5.7 convolution_convert_fusion
  634.7 12.6 %copy.27 = bf16[32,192,768]{2,1,0:T(8,128)(2,1)} copy(bf16[32,192,768]{2,0,1:T(8,128)(2,1)} %convolution_convert_fusion) | data formatting | bytes 18874368 | tf_op jit(solution)/shard_map/convert_element_type | solution.py:41
  647.3 7.7 all-to-all-start
  655.0 0.0 copy-start.1
  655.0 2.7 slice_bitcast_fusion
  657.8 109.8 %all-to-all-done = bf16[32,192,768]{2,1,0:T(8,128)(2,1)} async-done(((bf16[32,192,768]{2,1,0:T(8,128)(2,1)}), bf16[32,192,768]{2,1,0:T(8,128)(2,1)}, u32[]{:S(2)}, u32[]{:S(2)}) %all-to-all-start) | async-done | bytes 9437216 | tf_op jit(solution)/shard_map/all_to_all | solution.py:44
  767.5 5.9 reduce_sum.12
  (4 shorter events, 0.0 us)
Async XLA Ops:
  7.2 171.1 %copy-start = (bf16[5,256,1024]{2,1,0:T(8,128)(2,1)S(1)}, bf16[5,256,1024]{2,1,0:T(8,128)(2,1)}, u32[]{:S(2)}) copy-start(bf16[5,256,1024]{2,1,0:T(8,128)(2,1)} %param.4) | copy-start | bytes 7864324
  7.2 171.0 %all-gather.2.cloned.1.call-start = ((), (), s32[]{:S(2)}) async-start(), calls=%async_computation.2 | async-start | bytes 19660800 | tf_op jit(solution)/shard_map/all_gather | solution.py:27
  26.3 586.2 %reduce-scatter.4.cloned.1.call-start = ((), (), s32[]{:S(2)}) async-start(), calls=%async_computation.3 | async-start | bytes 44236800
  189.9 4.0 copy-start.2
  313.6 0.7 copy-start.4
  626.7 2.1 copy-start.3
  647.3 120.2 %all-to-all-start = ((bf16[32,192,768]{2,1,0:T(8,128)(2,1)}), bf16[32,192,768]{2,1,0:T(8,128)(2,1)}, u32[]{:S(2)}, u32[]{:S(2)}) async-start(bf16[32,192,768]{2,1,0:T(8,128)(2,1)} %copy.27), calls=%async_computation | async-start | bytes 18874368 | tf_op jit(solution)/shard_map/all_to_all | solution.py:44
  655.0 118.5 %copy-start.1 = (bf16[5,256,1024]{2,1,0:T(8,128)(2,1)S(1)}, bf16[5,256,1024]{2,1,0:T(8,128)(2,1)}, u32[]{:S(2)}) copy-start(bf16[5,256,1024]{2,1,0:T(8,128)(2,1)} %param.4) | copy-start | bytes 7864324
Sparse Core Ops, SparseCore 0:
  26.4 151.7 all-gather.1
  313.7 298.7 reduce-scatter.3
where the time goes:
time: 789 us; the launch traced here: 780 us
  waiting for transfers between devices  560 us (71%)
  local copies, waits for them, and re-layouts  135 us (17%)
  matrix products  32.4 us (4%)
  other arithmetic  31.6 us (4%)
  between operations  14.1 us (2%)
    unnamed x3, waiting for transfers between devices  298 us
    all_gather x1, waiting for transfers between devices, per_device(): lax.all_gather(projected, 'row', axis=1, tiled=True)  152 us
    all_to_all x1, waiting for transfers between devices, per_device(): lax.all_to_all(outgoing, 'col', split_axis=0, concat_axis=0, tiled=True)  110 us
    unnamed x14, local copies, waits for them, and re-layouts  105 us
    another operation x1, other arithmetic, pair_fills(): return jnp.stack((fill_aa, fill_bb, fill_ab), axis=2)  17 us
  transfers between devices with their start and end apart: 3, of which 3 were waited for; matrix products, arithmetic and copies ran while one was open for 0% of the time, Pallas kernels for 0%

commit v1 on v0

v1 whole, which is shorter than its diff:
```python
import functools

import jax
import jax.numpy as jnp
from jax import lax
from jax.experimental import pallas as pl
from jax.experimental.pallas import tpu as pltpu
from jax.sharding import PartitionSpec as P

MESH = pl.DeviceIdType.MESH
F32 = jnp.float32
BF16 = jnp.bfloat16
ROWS = 4
NB = 5
QN = 256
NS = 1024
FW = 768
QF = FW // ROWS
HF = QF // 2
HC = FW // 2
NONE = 4 * NB


def kernel(
    stiff, coup, inv, table,
    cross, diag,
    kbuf, pbuf, cin, ploc, left, fills, terms, dense, got1, part, got2, last, idx_v, idx_s,
    k_send, k_recv, c_sem, p_send, p_recv, t_send, t_recv, x_send, x_recv,
    s1_send, s1_recv, s2_send, s2_recv, f_send, f_recv, i_sem, i_send, i_recv,
):
    r = lax.axis_index("row")
    c = lax.axis_index("col")
    core = lax.rem(c, 2)
    y = lax.rem(c // 2, 4)
    z = c // 8
    other = c + 1 - 2 * core
    target = 2 * core

    def at_y(v):
        return z * 8 + v * 2 + core

    def at_z(v):
        return v * 8 + y * 2 + core

    def wait(ref, sem):
        pltpu.make_async_copy(ref, ref, sem).wait()

    def remote(src, dst, send, recv, device):
        return pltpu.make_async_remote_copy(
            src_ref=src, dst_ref=dst, send_sem=send, recv_sem=recv, device_id=device, device_id_type=MESH
        )

    order = [4] + [lax.rem(r + d, ROWS) for d in (1, 2, 3, 0)]
    loads = [pltpu.make_async_copy(coup.at[b], cin.at[b], c_sem.at[i]) for i, b in enumerate(order)]
    for load in loads:
        load.start()

    barrier = pltpu.get_barrier_semaphore()
    partners = [(r, other)]
    for d in (1, 2, 3):
        row = lax.rem(r + d, ROWS)
        partners += [(row, c), (row, other), (r, at_y(lax.rem(y + d, 4))), (r, at_z(lax.rem(z + d, 4)))]
    for device in partners:
        pl.semaphore_signal(barrier, inc=1, device_id=device, device_id_type=MESH)
    pl.semaphore_wait(barrier, len(partners))

    mine = pl.ds(pl.multiple_of(r * QN, QN), QN)

    def k_copy(i, b, slot, row):
        return remote(stiff.at[b], kbuf.at[slot, mine], k_send.at[i], k_recv.at[slot, r], (row, c))

    def k_local(b, slot):
        return pltpu.make_async_copy(stiff.at[b], kbuf.at[slot, mine], k_recv.at[slot, r])

    def p_copy(i, b, slot, row, k):
        return remote(
            ploc.at[b, pl.ds(k * FW, FW)], pbuf.at[slot, pl.ds(k * FW, FW), mine],
            p_send.at[i, k], p_recv.at[slot, r, k], (row, c),
        )

    def p_local(b, slot, k):
        return pltpu.make_async_copy(
            ploc.at[b, pl.ds(k * FW, FW)], pbuf.at[slot, pl.ds(k * FW, FW), mine], p_recv.at[slot, r, k]
        )

    def send_block(i, remote_copy, local_copy):
        if i == 0:
            @pl.when(r == target)
            def _():
                local_copy(4, 0).start()

            @pl.when(r != target)
            def _():
                remote_copy(0, 4, 0, target).start()
        elif i < 4:
            remote_copy(i, order[i], 1, order[i]).start()
        else:
            local_copy(order[i], 1).start()

    for i in range(NB):
        send_block(i, k_copy, k_local)

    own_idx = pltpu.make_async_copy(table, idx_v.at[core], i_sem.at[0])
    own_idx.start()
    idx_copy = remote(table, idx_v.at[core], i_send, i_recv, (r, other))
    idx_copy.start()

    for i, b in enumerate(order):
        loads[i].wait()
        for k in range(2):
            raw = cin[b, :, k, :].astype(F32).T
            ploc[b, pl.ds(k * FW, FW), :] = (raw / inv[b]).astype(BF16)
            send_block(i, functools.partial(p_copy, k=k), functools.partial(p_local, k=k))

    terms[NONE] = jnp.zeros((HF, FW), BF16)
    own_idx.wait()
    idx_copy.wait()
    to_smem = pltpu.make_async_copy(idx_v, idx_s, i_sem.at[1])
    to_smem.start()
    to_smem.wait()

    def t_copies(slot, b, f, local=True):
        at = core * 2 * NB + b * 2 + f
        copies = []
        for dq in range(ROWS):
            for dh in range(2):
                q, h = lax.rem(r + dq, ROWS), lax.rem(core + dh, 2)
                src = fills.at[slot, f, pl.ds(pl.multiple_of(q * QF + h * HF, HF), HF)]
                if dq or dh:
                    copies.append(remote(
                        src, terms.at[at], t_send.at[slot, f, dq * 2 + dh], t_recv.at[at],
                        (q, c - core + h),
                    ))
                elif local:
                    copies.append(pltpu.make_async_copy(src, terms.at[at], t_recv.at[at]))
        return copies

    def x_copies(slot, b, local=True):
        copies = []
        for dq in range(ROWS):
            q = lax.rem(r + dq, ROWS)
            src = fills.at[slot, 2, pl.ds(pl.multiple_of(q * QF, QF), QF)]
            if dq:
                copies.append(remote(src, cross.at[b], x_send.at[slot, dq], x_recv.at[b], (q, c)))
            elif local:
                copies.append(pltpu.make_async_copy(src, cross.at[b], x_recv.at[b]))
        return copies

    def fill(slot, f, a, b):
        for n in range(3):
            out = lax.dot_general(
                left[a], pbuf[slot, pl.ds(b * FW + n * 256, 256), :],
                (((1,), (1,)), ((), ())), preferred_element_type=F32,
            )
            fills[slot, f, :, pl.ds(n * 256, 256)] = out.astype(BF16)

    def block(slot, unused):
        b = jnp.where(slot == 0, 4, r)
        for j in range(ROWS):
            wait(kbuf.at[slot, pl.ds(j * QN, QN)], k_recv.at[slot, j])
        for k in range(2):
            for j in range(ROWS):
                wait(pbuf.at[slot, pl.ds(k * FW, FW), pl.ds(j * QN, QN)], p_recv.at[slot, j, k])
            for n in range(4):
                out = jnp.dot(
                    pbuf[slot, pl.ds(k * FW, FW), :], kbuf[slot, :, pl.ds(n * 256, 256)],
                    preferred_element_type=F32,
                )
                left[k, :, pl.ds(n * 256, 256)] = out.astype(BF16)
            fill(slot, k, k, k)
            for copy in t_copies(slot, b, k):
                copy.start()
        fill(slot, 2, 0, 1)
        for copy in x_copies(slot, b):
            copy.start()
        return unused

    lax.fori_loop(jnp.where(r == target, 0, 1), 2, block, 0)

    for at in range(NONE):
        wait(terms.at[at], t_recv.at[at])

    def sum_terms(half, lead, cols):
        def one(j, unused):
            o, h = j // 2, lax.rem(j, 2)
            zz, yy = (o, lead) if half == 0 else (lead, o)
            m = zz * 8 + yy * 2 + h
            total = terms[idx_s[0, 0, m], :, cols].astype(F32) + terms[idx_s[0, 1, m], :, cols].astype(F32)
            total += terms[idx_s[1, 0, m], :, cols].astype(F32) + terms[idx_s[1, 1, m], :, cols].astype(F32)
            dense[half, lead, o, h] = total.astype(BF16)
            return unused

        lax.fori_loop(0, 8, one, 0)

    place = (y, z)
    whom = (at_y, at_z)
    columns = (pl.ds(0, HC), pl.ds(HC, HC))
    first = [[None] * 4, [None] * 4]
    for d in (2, 1, 3, 0):
        for half in range(2):
            lead = lax.rem(place[half] + d, 4)
            sum_terms(half, lead, columns[half])
            if d:
                copy = remote(
                    dense.at[half, lead], got1.at[half, d - 1],
                    s1_send.at[half, d - 1], s1_recv.at[half, d - 1], (r, whom[half](lead)),
                )
                copy.start()
                first[half][d] = copy

    second = [[None] * 4, [None] * 4]
    for half in range(2):
        for d in (1, 2, 3):
            first[half][d].wait_recv()
        for d in (2, 1, 3, 0):
            o = lax.rem(place[1 - half] + d, 4)
            total = dense[half, place[half], o].astype(F32)
            for e in range(3):
                total += got1[half, e, o].astype(F32)
            part[half, o] = total.astype(BF16)
            if d:
                copy = remote(
                    part.at[half, o], got2.at[half, d - 1],
                    s2_send.at[half, d - 1], s2_recv.at[half, d - 1], (r, whom[1 - half](o)),
                )
                copy.start()
                second[half][d] = copy

    for half in range(2):
        for d in (1, 2, 3):
            second[half][d].wait_recv()
        total = part[half, place[1 - half]].astype(F32)
        for e in range(3):
            total += got2[half, e].astype(F32)
        last[:, :, columns[half]] = total.astype(BF16)

    own_rows = pl.ds(pl.multiple_of(core * HF, HF), HF)
    keep = pltpu.make_async_copy(last.at[core], diag.at[0, own_rows], f_recv.at[core])
    keep.start()
    give = remote(last.at[1 - core], diag.at[0, own_rows], f_send, f_recv.at[core], (r, other))
    give.start()

    for b in range(NB):
        wait(cross.at[b], x_recv.at[b])
    for h in range(2):
        wait(diag.at[0, pl.ds(h * HF, HF)], f_recv.at[h])
    give.wait_send()
    for half in range(2):
        for d in (1, 2, 3):
            first[half][d].wait_send()
            second[half][d].wait_send()

    @pl.when(r != target)
    def _():
        k_copy(0, 4, 0, target).wait_send()
        for k in range(2):
            p_copy(0, 4, 0, target, k).wait_send()

    for i in (1, 2, 3):
        k_copy(i, order[i], 1, order[i]).wait_send()
        for k in range(2):
            p_copy(i, order[i], 1, order[i], k).wait_send()

    def drain(slot, unused):
        b = jnp.where(slot == 0, 4, r)
        for f in range(2):
            for copy in t_copies(slot, b, f, False):
                copy.wait_send()
        for copy in x_copies(slot, b, False):
            copy.wait_send()
        return unused

    lax.fori_loop(jnp.where(r == target, 0, 1), 2, drain, 0)


def per_device(stiffness, coupling, slave_diag, slave_masters):
    core = lax.rem(lax.axis_index("col"), 2)
    refs = jnp.arange(2 * NB, dtype=jnp.int32)
    hit = slave_masters.reshape(1, 2 * NB) == jnp.arange(128, dtype=jnp.int32)[:, None]
    low = jnp.min(jnp.where(hit, refs, 2 * NB), axis=1)
    high = jnp.max(jnp.where(hit, refs, -1), axis=1)
    base = core * 2 * NB
    table = jnp.stack((
        jnp.where(high >= 0, low + base, NONE),
        jnp.where(high > low, high + base, NONE),
    ))
    table = jnp.pad(table, ((0, 6), (0, 0))).astype(jnp.int32)
    any_space = pl.BlockSpec(memory_space=pl.ANY)
    vmem = pl.BlockSpec(memory_space=pltpu.VMEM)
    dma = pltpu.SemaphoreType.DMA
    flops = 2 * NB * (2 * NS * NS * FW + 3 * FW * FW * NS) // 4
    return pl.pallas_call(
        kernel,
        out_shape=(
            jax.ShapeDtypeStruct((NB, QF, FW), BF16),
            jax.ShapeDtypeStruct((1, QF, FW), BF16),
        ),
        in_specs=[any_space, any_space, vmem, vmem],
        out_specs=(any_space, any_space),
        scratch_shapes=[
            pltpu.VMEM((2, NS, NS), BF16),
            pltpu.VMEM((2, 2 * FW, NS), BF16),
            pltpu.VMEM((NB, QN, 2, FW), BF16),
            pltpu.VMEM((NB, 2 * FW, QN), BF16),
            pltpu.VMEM((2, FW, NS), BF16),
            pltpu.VMEM((2, 3, FW, FW), BF16),
            pltpu.VMEM((NONE + 1, HF, FW), BF16),
            pltpu.VMEM((2, 4, 4, 2, HF, HC), BF16),
            pltpu.VMEM((2, 3, 4, 2, HF, HC), BF16),
            pltpu.VMEM((2, 4, 2, HF, HC), BF16),
            pltpu.VMEM((2, 3, 2, HF, HC), BF16),
            pltpu.VMEM((2, HF, FW), BF16),
            pltpu.VMEM((2, 8, 128), jnp.int32),
            pltpu.SMEM((2, 8, 128), jnp.int32),
            dma((NB,)), dma((2, ROWS)), dma((NB,)), dma((NB, 2)), dma((2, ROWS, 2)),
            dma((2, 2, 8)), dma((NONE,)), dma((2, ROWS)), dma((NB,)),
            dma((2, 3)), dma((2, 3)), dma((2, 3)), dma((2, 3)), dma, dma((2,)), dma((2,)), dma, dma,
        ],
        compiler_params=pltpu.CompilerParams(
            collective_id=0, has_side_effects=True, vmem_limit_bytes=58 * 2**20
        ),
        cost_estimate=pl.CostEstimate(flops=flops, bytes_accessed=9 * 2**20, transcendentals=0),
        name="condense",
    )(stiffness, coupling, slave_diag.reshape(NB, 1, QN), table)


def solution(mesh):
    return jax.shard_map(
        per_device,
        mesh=mesh,
        in_specs=(
            P("col", "row", None),
            P("col", "row", None, None),
            P("col", "row"),
            P("col", None),
        ),
        out_specs=(P("col", "row", None), P("col", "row", None)),
        check_vma=False,
    )
```

time: 789 us -> 184 us (0.23); the launches traced: 780 us -> 183 us
  waiting for transfers between devices: 560 us -> 0 us
  Pallas kernels: 0 us -> 176 us
  local copies, waits for them, and re-layouts: 135 us -> 6.08 us
  matrix products: 32.4 us -> 0 us
  other arithmetic: 31.6 us -> 0.11 us
  between operations: 14.1 us -> 0.66 us
    unnamed x3 -> x0, waiting for transfers between devices: 298 us -> none
    pallas_call x0 -> x1, Pallas kernels: none -> 176 us  [per_device(): pl.pallas_call(kernel, out_shape=(jax.ShapeDtypeStruct((NB, QF, FW), BF16...]
    all_gather x1 -> x0, waiting for transfers between devices: 152 us -> none  [per_device(): lax.all_gather(projected, 'row', axis=1, tiled=True)]
    all_to_all x1 -> x0, waiting for transfers between devices: 110 us -> none  [per_device(): lax.all_to_all(outgoing, 'col', split_axis=0, concat_axis=0, tiled=True)]
    unnamed x14 -> x5, local copies, waits for them, and re-layouts: 105 us -> 4.11 us
    dot_general x5 -> x0, matrix products: 32.4 us -> none  [the longest x1 11.7 us: per_device(): jnp.einsum('srk,skc->src', stiffness, lax.all_gather(projected, 'row', ax...]
    convert_element_type x2 -> x0, local copies, waits for them, and re-layouts: 23 us -> none  [the longest x1 12.6 us: per_device(): jnp.einsum('rec,ep->prc', terms, onehot, preferred_element_type=jnp.float32)]
    another operation x1, other arithmetic: 17 us -> 0.01 us  [per_device(): jnp.stack((jnp.where(high >= 0, low + base, NONE), jnp.where(high > low,...]
  transfers between devices with their start and end apart: 3 -> 0, of which waited for: 3 -> 0; matrix products, arithmetic and copies ran while one was open for 0% -> 0% of each run, Pallas kernels for 0% -> 0%
where the time goes in v1:
time: 184 us; the launch traced here: 183 us
  Pallas kernels  176 us (96%)
  local copies, waits for them, and re-layouts  6.08 us (3%)
    pallas_call x1, Pallas kernels, per_device(): pl.pallas_call(kernel, out_shape=(jax.ShapeDtypeStruct((NB, QF, FW), BF16...  176 us
    unnamed x5, local copies, waits for them, and re-layouts  4.11 us

profile of v1, /device:TPU:1, one launch (start us, length us, event | category | flops | bytes accessed | tf_op | source)
XLA Modules:
  0.0 183.3 jit_solution(13843656811226075676)
XLA Ops:
  0.6 0.8 copy.8
  1.4 0.1 eq.15
  1.5 0.1 select_reduce_fusion
  1.6 0.6 pad.4.table
  2.2 1.3 reshape.54.inv
  3.5 176.4 %condense.1 = (bf16[5,192,768]{2,1,0:T(8,128)(2,1)}, bf16[1,192,768]{2,1,0:T(8,128)(2,1)}) custom-call(bf16[5,256,1024]{2,1,0:T(8,128)(2,1)} %stiff.1, bf16[5,256,2,768]{3,2,1,0:T(2,128)(2,1)} %coup.1, f32[5,1,256]{2,1,0:T(1,128)} %reshape.54.inv, s32[8,128]{1,0:T(8,128)} %pad.4.table), custom_call_target="tpu_custom_call" | custom-call | flops 8556380160 | bytes 9437184 | tf_op jit(solution)/shard_map/condense/pallas_call | solution.py:292
  179.9 0.0 copy-start
  179.9 2.6 %copy.11 = bf16[5,192,768]{2,1,0:T(8,128)(2,1)} copy(bf16[5,192,768]{2,1,0:T(8,128)(2,1)} %get-tuple-element.8) | data formatting | bytes 2949120
  182.5 0.0 copy-done
  182.5 0.7 copy.12
  (2 shorter events, 0.0 us)
Async XLA Ops:
  179.9 2.6 %copy-start = (bf16[1,192,768]{2,1,0:T(8,128)(2,1)S(1)}, bf16[1,192,768]{2,1,0:T(8,128)(2,1)}, u32[]{:S(2)}) copy-start(bf16[1,192,768]{2,1,0:T(8,128)(2,1)} %get-tuple-element.9) | copy-start | bytes 884740

commit v2 on v1

v2 whole, which is shorter than its diff:
```python
import functools

import jax
import jax.numpy as jnp
from jax import lax
from jax.experimental import pallas as pl
from jax.experimental.pallas import tpu as pltpu
from jax.sharding import PartitionSpec as P

MESH = pl.DeviceIdType.MESH
F32 = jnp.float32
BF16 = jnp.bfloat16
ROWS = 4
NB = 5
QN = 256
NS = 1024
FW = 768
QF = FW // ROWS
HF = QF // 2
HC = FW // 2
NONE = 4 * NB
CH = 3
CR = HF // CH


def kernel(
    stiff, coup, scale, masters,
    cross, diag,
    kbuf, pbuf, cin, ploc, left, fills, terms0, terms1, terms2, dense, got1, part, got2, last, own_table, idx_v, idx_s,
    k_send, k_recv, c_sem, p_send, p_recv, t_send, t_recv, x_send, x_recv,
    s1_send, s1_recv, s2_send, s2_recv, f_send, f_recv, i_sem, i_send, i_recv,
):
    r = lax.axis_index("row")
    c = lax.axis_index("col")
    terms = (terms0, terms1, terms2)
    core = lax.rem(c, 2)
    y = lax.rem(c // 2, 4)
    z = c // 8
    other = c + 1 - 2 * core
    target = 2 * core

    def at_y(v):
        return z * 8 + v * 2 + core

    def at_z(v):
        return v * 8 + y * 2 + core

    def wait(ref, sem):
        pltpu.make_async_copy(ref, ref, sem).wait()

    def remote(src, dst, send, recv, device):
        return pltpu.make_async_remote_copy(
            src_ref=src, dst_ref=dst, send_sem=send, recv_sem=recv, device_id=device, device_id_type=MESH
        )

    order = [4] + [lax.rem(r + d, ROWS) for d in (1, 2, 3, 0)]
    loads = [pltpu.make_async_copy(coup.at[b], cin.at[b], c_sem.at[i]) for i, b in enumerate(order)]
    for load in loads:
        load.start()

    lane = lax.broadcasted_iota(jnp.int32, (8, 128), 1)
    low, high = jnp.full((8, 128), NONE, jnp.int32), jnp.full((8, 128), -1, jnp.int32)
    for e in range(2 * NB):
        hit = lane == jnp.broadcast_to(masters[pl.ds(e % 2, 1), pl.ds(e // 2, 1)], (8, 128))
        low = jnp.minimum(low, jnp.where(hit, core * 2 * NB + e, NONE))
        high = jnp.maximum(high, jnp.where(hit, core * 2 * NB + e, -1))
    own_table[0] = low
    own_table[1] = jnp.where(high > low, high, NONE)

    barrier = pltpu.get_barrier_semaphore()
    partners = [(r, other)]
    for d in (1, 2, 3):
        row = lax.rem(r + d, ROWS)
        partners += [(row, c), (row, other), (r, at_y(lax.rem(y + d, 4))), (r, at_z(lax.rem(z + d, 4)))]
    for device in partners:
        pl.semaphore_signal(barrier, inc=1, device_id=device, device_id_type=MESH)
    pl.semaphore_wait(barrier, len(partners))

    mine = pl.ds(pl.multiple_of(r * QN, QN), QN)

    def k_copy(i, b, slot, row):
        return remote(stiff.at[b], kbuf.at[slot, mine], k_send.at[i], k_recv.at[slot, r], (row, c))

    def k_local(b, slot):
        return pltpu.make_async_copy(stiff.at[b], kbuf.at[slot, mine], k_recv.at[slot, r])

    def p_copy(i, b, slot, row, k):
        return remote(
            ploc.at[b, pl.ds(k * FW, FW)], pbuf.at[slot, pl.ds(k * FW, FW), mine],
            p_send.at[i, k], p_recv.at[slot, r, k], (row, c),
        )

    def p_local(b, slot, k):
        return pltpu.make_async_copy(
            ploc.at[b, pl.ds(k * FW, FW)], pbuf.at[slot, pl.ds(k * FW, FW), mine], p_recv.at[slot, r, k]
        )

    def send_block(i, remote_copy, local_copy):
        if i == 0:
            @pl.when(r == target)
            def _():
                local_copy(4, 0).start()

            @pl.when(r != target)
            def _():
                remote_copy(0, 4, 0, target).start()
        elif i < 4:
            remote_copy(i, order[i], 1, order[i]).start()
        else:
            local_copy(order[i], 1).start()

    for i in range(NB):
        send_block(i, k_copy, k_local)

    own_idx = pltpu.make_async_copy(own_table, idx_v.at[core], i_sem.at[0])
    own_idx.start()
    idx_copy = remote(own_table, idx_v.at[core], i_send, i_recv, (r, other))
    idx_copy.start()

    for i, k in [(0, 0), (0, 1)] + [(i, k) for k in range(2) for i in range(1, NB)]:
        b = order[i]
        if k == 0:
            loads[i].wait()
        raw = cin[b, :, k, :].astype(F32).T
        ploc[b, pl.ds(k * FW, FW), :] = (raw / scale[pl.ds(b, 1), :]).astype(BF16)
        send_block(i, functools.partial(p_copy, k=k), functools.partial(p_local, k=k))

    for chunk in terms:
        chunk[NONE] = jnp.zeros((CR, FW), BF16)
    own_idx.wait()
    idx_copy.wait()
    to_smem = pltpu.make_async_copy(idx_v, idx_s, i_sem.at[1])
    to_smem.start()
    to_smem.wait()

    def t_copies(slot, b, f, j, local=True):
        at = core * 2 * NB + b * 2 + f
        copies = []
        for dq in range(ROWS):
            for dh in range(2):
                q, h = lax.rem(r + dq, ROWS), lax.rem(core + dh, 2)
                src = fills.at[slot, f, pl.ds(pl.multiple_of(q * QF + h * HF + j * CR, CR), CR)]
                dst = terms[j].at[at]
                if dq or dh:
                    copies.append(remote(
                        src, dst, t_send.at[slot, f, j, dq * 2 + dh], t_recv.at[j, at], (q, c - core + h)
                    ))
                elif local:
                    copies.append(pltpu.make_async_copy(src, dst, t_recv.at[j, at]))
        return copies

    def x_copies(slot, b, local=True):
        copies = []
        for dq in range(ROWS):
            q = lax.rem(r + dq, ROWS)
            src = fills.at[slot, 2, pl.ds(pl.multiple_of(q * QF, QF), QF)]
            if dq:
                copies.append(remote(src, cross.at[b], x_send.at[slot, dq], x_recv.at[b], (q, c)))
            elif local:
                copies.append(pltpu.make_async_copy(src, cross.at[b], x_recv.at[b]))
        return copies

    def fill(slot, f, a, b):
        for n in range(3):
            out = lax.dot_general(
                left[a], pbuf[slot, pl.ds(b * FW + n * 256, 256), :],
                (((1,), (1,)), ((), ())), preferred_element_type=F32,
            )
            fills[slot, f, :, pl.ds(n * 256, 256)] = out.astype(BF16)

    def multiply(slot, k):
        for n in range(4):
            out = jnp.dot(
                pbuf[slot, pl.ds(k * FW, FW), :], kbuf[slot, :, pl.ds(n * 256, 256)],
                preferred_element_type=F32,
            )
            left[k, :, pl.ds(n * 256, 256)] = out.astype(BF16)

    def block(slot, unused):
        b = jnp.where(slot == 0, 4, r)

        def p_wait(k):
            for j in range(ROWS):
                wait(pbuf.at[slot, pl.ds(k * FW, FW), pl.ds(j * QN, QN)], p_recv.at[slot, j, k])

        def t_start(f, j):
            for copy in t_copies(slot, b, f, j):
                copy.start()

        for j in range(ROWS):
            wait(kbuf.at[slot, pl.ds(j * QN, QN)], k_recv.at[slot, j])
        p_wait(0)
        multiply(slot, 0)
        fill(slot, 0, 0, 0)
        p_wait(1)
        t_start(0, 0)
        t_start(0, 1)
        multiply(slot, 1)
        fill(slot, 1, 1, 1)
        t_start(1, 0)
        t_start(1, 1)
        t_start(0, 2)
        t_start(1, 2)
        fill(slot, 2, 0, 1)
        for copy in x_copies(slot, b):
            copy.start()
        return unused

    lax.fori_loop(jnp.where(r == target, 0, 1), 2, block, 0)

    place = (y, z)
    whom = (at_y, at_z)
    columns = (pl.ds(0, HC), pl.ds(HC, HC))

    def sum_terms(j, half, lead):
        chunk, cols = terms[j], columns[half]

        def one(n, unused):
            o, h = n // 2, lax.rem(n, 2)
            zz, yy = (o, lead) if half == 0 else (lead, o)
            m = zz * 8 + yy * 2 + h
            total = chunk[idx_s[0, 0, 0, m], :, cols].astype(F32) + chunk[idx_s[0, 1, 0, m], :, cols].astype(F32)
            total += chunk[idx_s[1, 0, 0, m], :, cols].astype(F32) + chunk[idx_s[1, 1, 0, m], :, cols].astype(F32)
            dense[j, half, lead, o, h] = total.astype(BF16)
            return unused

        lax.fori_loop(0, 8, one, 0)

    def first_copy(j, half, d):
        lead = lax.rem(place[half] + d, 4)
        return remote(
            dense.at[j, half, lead], got1.at[j, half, d - 1],
            s1_send.at[j, half, d - 1], s1_recv.at[j, half, d - 1], (r, whom[half](lead)),
        )

    def second_copy(j, half, d):
        o = lax.rem(place[1 - half] + d, 4)
        return remote(
            part.at[j, half, o], got2.at[j, half, d - 1],
            s2_send.at[j, half, d - 1], s2_recv.at[j, half, d - 1], (r, whom[1 - half](o)),
        )

    def stage0(j):
        for at in range(NONE):
            wait(terms[j].at[at], t_recv.at[j, at])
        for d in (2, 1, 3, 0):
            for half in range(2):
                sum_terms(j, half, lax.rem(place[half] + d, 4))
                if d:
                    first_copy(j, half, d).start()

    def stage1(j):
        for half in range(2):
            for d in (1, 2, 3):
                first_copy(j, half, d).wait_recv()
            for d in (2, 1, 3, 0):
                o = lax.rem(place[1 - half] + d, 4)
                total = dense[j, half, place[half], o].astype(F32)
                for e in range(3):
                    total += got1[j, half, e, o].astype(F32)
                part[j, half, o] = total.astype(BF16)
                if d:
                    second_copy(j, half, d).start()

    def out_rows(j, h):
        return diag.at[0, pl.ds(pl.multiple_of(h * HF + j * CR, CR), CR)]

    def give(j):
        return remote(
            last.at[1 - core, pl.ds(j * CR, CR)], out_rows(j, core),
            f_send.at[j], f_recv.at[j, core], (r, other),
        )

    def stage2(j):
        rows = pl.ds(j * CR, CR)
        for half in range(2):
            for d in (1, 2, 3):
                second_copy(j, half, d).wait_recv()
            total = part[j, half, place[1 - half]].astype(F32)
            for e in range(3):
                total += got2[j, half, e].astype(F32)
            last[:, rows, columns[half]] = total.astype(BF16)
        pltpu.make_async_copy(last.at[core, rows], out_rows(j, core), f_recv.at[j, core]).start()
        give(j).start()

    stage0(0)
    stage0(1)
    stage1(0)
    stage0(2)
    stage1(1)
    stage2(0)
    stage1(2)
    stage2(1)
    stage2(2)

    for b in range(NB):
        wait(cross.at[b], x_recv.at[b])
    for j in range(CH):
        for h in range(2):
            wait(out_rows(j, h), f_recv.at[j, h])
        give(j).wait_send()
        for half in range(2):
            for d in (1, 2, 3):
                first_copy(j, half, d).wait_send()
                second_copy(j, half, d).wait_send()

    @pl.when(r != target)
    def _():
        k_copy(0, 4, 0, target).wait_send()
        for k in range(2):
            p_copy(0, 4, 0, target, k).wait_send()

    for i in (1, 2, 3):
        k_copy(i, order[i], 1, order[i]).wait_send()
        for k in range(2):
            p_copy(i, order[i], 1, order[i], k).wait_send()

    def drain(slot, unused):
        b = jnp.where(slot == 0, 4, r)
        for f in range(2):
            for j in range(CH):
                for copy in t_copies(slot, b, f, j, False):
                    copy.wait_send()
        for copy in x_copies(slot, b, False):
            copy.wait_send()
        return unused

    lax.fori_loop(jnp.where(r == target, 0, 1), 2, drain, 0)


def per_device(stiffness, coupling, slave_diag, slave_masters):
    any_space = pl.BlockSpec(memory_space=pl.ANY)
    vmem = pl.BlockSpec(memory_space=pltpu.VMEM)
    dma = pltpu.SemaphoreType.DMA
    flops = 2 * NB * (2 * NS * NS * FW + 3 * FW * FW * NS) // 4
    return pl.pallas_call(
        kernel,
        out_shape=(
            jax.ShapeDtypeStruct((NB, QF, FW), BF16),
            jax.ShapeDtypeStruct((1, QF, FW), BF16),
        ),
        in_specs=[any_space, any_space, vmem, vmem],
        out_specs=(any_space, any_space),
        scratch_shapes=[
            pltpu.VMEM((2, NS, NS), BF16),
            pltpu.VMEM((2, 2 * FW, NS), BF16),
            pltpu.VMEM((NB, QN, 2, FW), BF16),
            pltpu.VMEM((NB, 2 * FW, QN), BF16),
            pltpu.VMEM((2, FW, NS), BF16),
            pltpu.VMEM((2, 3, FW, FW), BF16),
            *[pltpu.VMEM((NONE + 1, CR, FW), BF16)] * CH,
            pltpu.VMEM((CH, 2, 4, 4, 2, CR, HC), BF16),
            pltpu.VMEM((CH, 2, 3, 4, 2, CR, HC), BF16),
            pltpu.VMEM((CH, 2, 4, 2, CR, HC), BF16),
            pltpu.VMEM((CH, 2, 3, 2, CR, HC), BF16),
            pltpu.VMEM((2, HF, FW), BF16),
            pltpu.VMEM((2, 8, 128), jnp.int32),
            pltpu.VMEM((2, 2, 8, 128), jnp.int32),
            pltpu.SMEM((2, 2, 8, 128), jnp.int32),
            dma((NB,)), dma((2, ROWS)), dma((NB,)), dma((NB, 2)), dma((2, ROWS, 2)),
            dma((2, 2, CH, 8)), dma((CH, NONE)), dma((2, ROWS)), dma((NB,)),
            dma((CH, 2, 3)), dma((CH, 2, 3)), dma((CH, 2, 3)), dma((CH, 2, 3)),
            dma((CH,)), dma((CH, 2)), dma((2,)), dma, dma,
        ],
        compiler_params=pltpu.CompilerParams(
            collective_id=0, has_side_effects=True, vmem_limit_bytes=58 * 2**20
        ),
        cost_estimate=pl.CostEstimate(flops=flops, bytes_accessed=9 * 2**20, transcendentals=0),
        name="condense",
    )(stiffness, coupling, slave_diag, slave_masters.T)


def solution(mesh):
    return jax.shard_map(
        per_device,
        mesh=mesh,
        in_specs=(
            P("col", "row", None),
            P("col", "row", None, None),
            P("col", "row"),
            P("col", None),
        ),
        out_specs=(P("col", "row", None), P("col", "row", None)),
        check_vma=False,
    )
```

time: 184 us -> 177 us (0.962)
  Pallas kernels: 176 us -> 171 us
  local copies, waits for them, and re-layouts: 6.08 us -> 3.34 us
    pallas_call x1, Pallas kernels: 176 us -> 171 us  [per_device(): pl.pallas_call(kernel, out_shape=(jax.ShapeDtypeStruct((NB, QF, FW), BF16...]
    unnamed x5 -> x4, local copies, waits for them, and re-layouts: 4.11 us -> 3.34 us
where the time goes in v2:
time: 177 us; the launch traced here: 175 us
  Pallas kernels  171 us (97%)
  local copies, waits for them, and re-layouts  3.34 us (2%)
    pallas_call x1, Pallas kernels, per_device(): pl.pallas_call(kernel, out_shape=(jax.ShapeDtypeStruct((NB, QF, FW), BF16...  171 us

profile of v2, /device:TPU:1, one launch (start us, length us, event | category | flops | bytes accessed | tf_op | source)
XLA Modules:
  0.0 175.5 jit_solution(362000542206699210)
XLA Ops:
  0.6 171.5 %condense.1 = (bf16[5,192,768]{2,1,0:T(8,128)(2,1)}, bf16[1,192,768]{2,1,0:T(8,128)(2,1)}) custom-call(bf16[5,256,1024]{2,1,0:T(8,128)(2,1)} %stiff.1, bf16[5,256,2,768]{3,2,1,0:T(2,128)(2,1)} %coup.1, f32[5,256]{1,0:T(8,128)} %scale.1, s32[2,5]{1,0:T(2,128)} %bitcast.1), custom_call_target="tpu_custom_call" | custom-call | flops 8556380160 | bytes 9437184 | tf_op jit(solution)/shard_map/condense/pallas_call | solution.py:336
  172.1 0.0 copy-start
  172.1 2.6 %copy.8 = bf16[5,192,768]{2,1,0:T(8,128)(2,1)} copy(bf16[5,192,768]{2,1,0:T(8,128)(2,1)} %get-tuple-element.4) | data formatting | bytes 2949120
  174.7 0.0 copy-done
  174.7 0.7 copy.9
Async XLA Ops:
  172.1 2.6 %copy-start = (bf16[1,192,768]{2,1,0:T(8,128)(2,1)S(1)}, bf16[1,192,768]{2,1,0:T(8,128)(2,1)}, u32[]{:S(2)}) copy-start(bf16[1,192,768]{2,1,0:T(8,128)(2,1)} %get-tuple-element.5) | copy-start | bytes 884740

commit v3 on v2

--- a/solution.py
+++ b/solution.py
@@ -26,24 +26,25 @@
 def kernel(
     stiff, coup, scale, masters,
     cross, diag,
-    kbuf, pbuf, cin, ploc, left, fills, terms0, terms1, terms2, dense, got1, part, got2, last, own_table, idx_v, idx_s,
-    k_send, k_recv, c_sem, p_send, p_recv, t_send, t_recv, x_send, x_recv,
-    s1_send, s1_recv, s2_send, s2_recv, f_send, f_recv, i_sem, i_send, i_recv,
+    kbuf, pbuf, cin, ploc, relay, left, fills, dense, got1, part, got2, last, own_table, idx_v, idx_s,
+    k_send, k_recv, c_sem, p_send, p_recv, r_send, r_recv, t_send, t_recv, x_send, x_recv,
+    s1_send, s1_recv, s2_send, s2_recv, f_sem, i_sem, i_send, i_recv, ready, *terms,
 ):
     r = lax.axis_index("row")
     c = lax.axis_index("col")
-    terms = (terms0, terms1, terms2)
     core = lax.rem(c, 2)
     y = lax.rem(c // 2, 4)
     z = c // 8
     other = c + 1 - 2 * core
     target = 2 * core
-
-    def at_y(v):
-        return z * 8 + v * 2 + core
-
-    def at_z(v):
-        return v * 8 + y * 2 + core
+    through = target + 1
+    far = lax.rem(target + 2, ROWS)
+
+    def at_y(v, h=core):
+        return z * 8 + v * 2 + h
+
+    def at_z(v, h=core):
+        return v * 8 + y * 2 + h
 
     def wait(ref, sem):
         pltpu.make_async_copy(ref, ref, sem).wait()
@@ -71,7 +72,9 @@
     partners = [(r, other)]
     for d in (1, 2, 3):
         row = lax.rem(r + d, ROWS)
-        partners += [(row, c), (row, other), (r, at_y(lax.rem(y + d, 4))), (r, at_z(lax.rem(z + d, 4)))]
+        partners += [(row, c), (row, other)]
+        for h in (core, 1 - core):
+            partners += [(r, at_y(lax.rem(y + d, 4), h)), (r, at_z(lax.rem(z + d, 4), h))]
     for device in partners:
         pl.semaphore_signal(barrier, inc=1, device_id=device, device_id_type=MESH)
     pl.semaphore_wait(barrier, len(partners))
@@ -90,40 +93,71 @@
             p_send.at[i, k], p_recv.at[slot, r, k], (row, c),
         )
 
+    def p_aside(k):
+        return remote(
+            ploc.at[4, pl.ds(k * FW, FW)], relay.at[pl.ds(k * FW, FW)],
+            p_send.at[0, k], r_recv.at[k], (through, c),
+        )
+
+    def p_forward(k):
+        return remote(
+            relay.at[pl.ds(k * FW, FW)],
+            pbuf.at[0, pl.ds(k * FW, FW), pl.ds(pl.multiple_of(far * QN, QN), QN)],
+            r_send.at[k], p_recv.at[0, far, k], (target, c),
+        )
+
     def p_local(b, slot, k):
         return pltpu.make_async_copy(
             ploc.at[b, pl.ds(k * FW, FW)], pbuf.at[slot, pl.ds(k * FW, FW), mine], p_recv.at[slot, r, k]
         )
 
-    def send_block(i, remote_copy, local_copy):
+    def send_block(i, remote_copy, local_copy, aside=None):
         if i == 0:
             @pl.when(r == target)
             def _():
                 local_copy(4, 0).start()
 
-            @pl.when(r != target)
+            @pl.when((r != target) & (r != far if aside else True))
             def _():
                 remote_copy(0, 4, 0, target).start()
+
+            if aside:
+                @pl.when(r == far)
+                def _():
+                    aside().start()
+        elif i == 3:
+            @pl.when(r != through)
+            def _():
+                remote_copy(i, order[i], 1, order[i]).start()
         elif i < 4:
             remote_copy(i, order[i], 1, order[i]).start()
         else:
             local_copy(order[i], 1).start()
 
-    for i in range(NB):
-        send_block(i, k_copy, k_local)
-
-    own_idx = pltpu.make_async_copy(own_table, idx_v.at[core], i_sem.at[0])
-    own_idx.start()
-    idx_copy = remote(own_table, idx_v.at[core], i_send, i_recv, (r, other))
-    idx_copy.start()
-
-    for i, k in [(0, 0), (0, 1)] + [(i, k) for k in range(2) for i in range(1, NB)]:
+    send_block(0, k_copy, k_local)
+
+    def project(i, k):
         b = order[i]
         if k == 0:
             loads[i].wait()
         raw = cin[b, :, k, :].astype(F32).T
         ploc[b, pl.ds(k * FW, FW), :] = (raw / scale[pl.ds(b, 1), :]).astype(BF16)
-        send_block(i, functools.partial(p_copy, k=k), functools.partial(p_local, k=k))
+        send_block(
+            i, functools.partial(p_copy, k=k), functools.partial(p_local, k=k), functools.partial(p_aside, k)
+        )
+
+    project(0, 0)
+    project(0, 1)
+    for i in range(1, NB):
+        send_block(i, k_copy, k_local)
+    for k in range(2):
+        for i in range(1, NB):
+            project(i, k)
+
+    own_idx = pltpu.make_async_copy(own_table, idx_v.at[core], i_sem.at[0])
+    own_idx.start()
+    idx_copy = remote(own_table, idx_v.at[core], i_send, i_recv, (r, other))
+    idx_copy.start()
 
     for chunk in terms:
         chunk[NONE] = jnp.zeros((CR, FW), BF16)
@@ -132,6 +166,15 @@
     to_smem = pltpu.make_async_copy(idx_v, idx_s, i_sem.at[1])
     to_smem.start()
     to_smem.wait()
+
+    @pl.when(r == through)
+    def _():
+        for k in range(2):
+            wait(relay.at[pl.ds(k * FW, FW)], r_recv.at[k])
+            p_forward(k).start()
+        k_copy(3, order[3], 1, order[3]).start()
+        for k in range(2):
+            p_copy(3, order[3], 1, order[3], k).start()
 
     def t_copies(slot, b, f, j, local=True):
         at = core * 2 * NB + b * 2 + f
@@ -187,26 +230,94 @@
             for copy in t_copies(slot, b, f, j):
                 copy.start()
 
-        for j in range(ROWS):
-            wait(kbuf.at[slot, pl.ds(j * QN, QN)], k_recv.at[slot, j])
+        def k_wait():
+            for j in range(ROWS):
+                wait(kbuf.at[slot, pl.ds(j * QN, QN)], k_recv.at[slot, j])
+
+        k_wait()
         p_wait(0)
         multiply(slot, 0)
         fill(slot, 0, 0, 0)
         p_wait(1)
-        t_start(0, 0)
-        t_start(0, 1)
+
+        @pl.when(owner & (slot == 1))
+        def _():
+            for device in ring:
+                pl.semaphore_signal(ready, inc=1, device_id=device, device_id_type=MESH)
+            t_start(0, 0)
+
         multiply(slot, 1)
         fill(slot, 1, 1, 1)
+
+        @pl.when(jnp.logical_not(owner))
+        def _():
+            fill(slot, 2, 0, 1)
+            pl.semaphore_wait(ready, 2)
+
+        @pl.when(jnp.logical_not(owner & (slot == 1)))
+        def _():
+            t_start(0, 0)
+
         t_start(1, 0)
-        t_start(1, 1)
-        t_start(0, 2)
-        t_start(1, 2)
-        fill(slot, 2, 0, 1)
-        for copy in x_copies(slot, b):
+        for j in range(1, CH):
+            for f in range(2):
+                t_start(f, j)
+
+        @pl.when(owner)
+        def _():
+            fill(slot, 2, 0, 1)
+
+        return unused
+
+    owner = r == target
+    def k_drain():
+        @pl.when(r != target)
+        def _():
+            k_copy(0, 4, 0, target).wait_send()
+
+        @pl.when((r != target) & (r != far))
+        def _():
+            for k in range(2):
+                p_copy(0, 4, 0, target, k).wait_send()
+
+        @pl.when(r == far)
+        def _():
+            for k in range(2):
+                p_aside(k).wait_send()
+
+        @pl.when(r == through)
+        def _():
+            for k in range(2):
+                p_forward(k).wait_send()
+
+        for i in (1, 2, 3):
+            k_copy(i, order[i], 1, order[i]).wait_send()
+            for k in range(2):
+                p_copy(i, order[i], 1, order[i], k).wait_send()
+
+    def t_drain(j):
+        def one(slot, unused):
+            for f in range(2):
+                for copy in t_copies(slot, jnp.where(slot == 0, 4, r), f, j, False):
+                    copy.wait_send()
+            return unused
+
+        lax.fori_loop(first_slot, 2, one, 0)
+
+    first_slot = jnp.where(owner, 0, 1)
+    ring = [(r, other)] + [(lax.rem(r + d, ROWS), col) for d in (1, 2, 3) for col in (c, other)]
+    lax.fori_loop(first_slot, 2, block, 0)
+    for copy in x_copies(1, r):
+        copy.start()
+
+    @pl.when(r == target)
+    def _():
+        for copy in x_copies(0, 4):
             copy.start()
-        return unused
-
-    lax.fori_loop(jnp.where(r == target, 0, 1), 2, block, 0)
+        pl.semaphore_wait(ready, 1)
+
+    k_drain()
+
 
     place = (y, z)
     whom = (at_y, at_z)
@@ -233,16 +344,31 @@
             s1_send.at[j, half, d - 1], s1_recv.at[j, half, d - 1], (r, whom[half](lead)),
         )
 
-    def second_copy(j, half, d):
+    def second_copies(j, half, d):
         o = lax.rem(place[1 - half] + d, 4)
-        return remote(
-            part.at[j, half, o], got2.at[j, half, d - 1],
-            s2_send.at[j, half, d - 1], s2_recv.at[j, half, d - 1], (r, whom[1 - half](o)),
-        )
-
-    def stage0(j):
+        return [
+            remote(
+                part.at[j, half, o, h], got2.at[j, half, d, core],
+                s2_send.at[j, half, d, e], s2_recv.at[j, half, d, core], (r, whom[1 - half](o, h)),
+            )
+            for e, h in ((0, core), (1, 1 - core)) if d or e
+        ]
+
+    def t_wait(j):
         for at in range(NONE):
             wait(terms[j].at[at], t_recv.at[j, at])
+
+    def first_wait(j, half):
+        for d in (1, 2, 3):
+            first_copy(j, half, d).wait_recv()
+
+    def second_wait(j, half):
+        for d in range(4):
+            for h in (1 - core, core) if d else (1 - core,):
+                wait(got2.at[j, half, d, h], s2_recv.at[j, half, d, h])
+
+    def stage0(j):
+        t_wait(j)
         for d in (2, 1, 3, 0):
             for half in range(2):
                 sum_terms(j, half, lax.rem(place[half] + d, 4))
@@ -250,82 +376,72 @@
                     first_copy(j, half, d).start()
 
     def stage1(j):
+        t_drain(j)
         for half in range(2):
-            for d in (1, 2, 3):
-                first_copy(j, half, d).wait_recv()
+            first_wait(j, half)
             for d in (2, 1, 3, 0):
                 o = lax.rem(place[1 - half] + d, 4)
                 total = dense[j, half, place[half], o].astype(F32)
                 for e in range(3):
                     total += got1[j, half, e, o].astype(F32)
                 part[j, half, o] = total.astype(BF16)
-                if d:
-                    second_copy(j, half, d).start()
-
-    def out_rows(j, h):
-        return diag.at[0, pl.ds(pl.multiple_of(h * HF + j * CR, CR), CR)]
-
-    def give(j):
-        return remote(
-            last.at[1 - core, pl.ds(j * CR, CR)], out_rows(j, core),
-            f_send.at[j], f_recv.at[j, core], (r, other),
-        )
+                for copy in second_copies(j, half, d):
+                    copy.start()
+            got2[j, half, 0, core] = part[j, half, place[1 - half], core]
+
+    def out_copy(j, h):
+        rows = pl.ds(h * HF + j * CR, CR)
+        return pltpu.make_async_copy(last.at[rows], diag.at[0, rows], f_sem.at[j, h])
 
     def stage2(j):
-        rows = pl.ds(j * CR, CR)
         for half in range(2):
             for d in (1, 2, 3):
-                second_copy(j, half, d).wait_recv()
-            total = part[j, half, place[1 - half]].astype(F32)
-            for e in range(3):
-                total += got2[j, half, e].astype(F32)
-            last[:, rows, columns[half]] = total.astype(BF16)
-        pltpu.make_async_copy(last.at[core, rows], out_rows(j, core), f_recv.at[j, core]).start()
-        give(j).start()
+                first_copy(j, half, d).wait_send()
+            if j:
+                for d in range(4):
+                    for copy in second_copies(j - 1, half, d):
+                        copy.wait_send()
+        for half in range(2):
+            second_wait(j, half)
+            total = got2[j, half, 0].astype(F32)
+            for d in (1, 2, 3):
+                total += got2[j, half, d].astype(F32)
+            total = total.astype(BF16)
+            for h in range(2):
+                last[pl.ds(h * HF + j * CR, CR), columns[half]] = total[h]
+        for h in range(2):
+            out_copy(j, h).start()
 
     stage0(0)
     stage0(1)
     stage1(0)
-    stage0(2)
-    stage1(1)
-    stage2(0)
-    stage1(2)
-    stage2(1)
-    stage2(2)
-
-    for b in range(NB):
-        wait(cross.at[b], x_recv.at[b])
+    for j in range(2, CH):
+        stage0(j)
+        stage1(j - 1)
+        stage2(j - 2)
+    stage1(CH - 1)
+    stage2(CH - 2)
+    stage2(CH - 1)
+
+    def x_wait():
+        for b in range(NB):
+            wait(cross.at[b], x_recv.at[b])
+
+    x_wait()
     for j in range(CH):
         for h in range(2):
-            wait(out_rows(j, h), f_recv.at[j, h])
-        give(j).wait_send()
+            out_copy(j, h).wait()
+    for d in range(4):
         for half in range(2):
-            for d in (1, 2, 3):
-                first_copy(j, half, d).wait_send()
-                second_copy(j, half, d).wait_send()
-
-    @pl.when(r != target)
-    def _():
-        k_copy(0, 4, 0, target).wait_send()
-        for k in range(2):
-            p_copy(0, 4, 0, target, k).wait_send()
-
-    for i in (1, 2, 3):
-        k_copy(i, order[i], 1, order[i]).wait_send()
-        for k in range(2):
-            p_copy(i, order[i], 1, order[i], k).wait_send()
-
-    def drain(slot, unused):
-        b = jnp.where(slot == 0, 4, r)
-        for f in range(2):
-            for j in range(CH):
-                for copy in t_copies(slot, b, f, j, False):
-                    copy.wait_send()
-        for copy in x_copies(slot, b, False):
+            for copy in second_copies(CH - 1, half, d):
+                copy.wait_send()
+
+    def x_drain(slot, unused):
+        for copy in x_copies(slot, jnp.where(slot == 0, 4, r), False):
             copy.wait_send()
         return unused
 
-    lax.fori_loop(jnp.where(r == target, 0, 1), 2, drain, 0)
+    lax.fori_loop(first_slot, 2, x_drain, 0)
 
 
 def per_device(stiffness, coupling, slave_diag, slave_masters):
@@ -346,21 +462,22 @@
             pltpu.VMEM((2, 2 * FW, NS), BF16),
             pltpu.VMEM((NB, QN, 2, FW), BF16),
             pltpu.VMEM((NB, 2 * FW, QN), BF16),
+            pltpu.VMEM((2 * FW, QN), BF16),
             pltpu.VMEM((2, FW, NS), BF16),
             pltpu.VMEM((2, 3, FW, FW), BF16),
-            *[pltpu.VMEM((NONE + 1, CR, FW), BF16)] * CH,
             pltpu.VMEM((CH, 2, 4, 4, 2, CR, HC), BF16),
             pltpu.VMEM((CH, 2, 3, 4, 2, CR, HC), BF16),
             pltpu.VMEM((CH, 2, 4, 2, CR, HC), BF16),
-            pltpu.VMEM((CH, 2, 3, 2, CR, HC), BF16),
-            pltpu.VMEM((2, HF, FW), BF16),
+            pltpu.VMEM((CH, 2, 4, 2, CR, HC), BF16),
+            pltpu.VMEM((QF, FW), BF16),
             pltpu.VMEM((2, 8, 128), jnp.int32),
             pltpu.VMEM((2, 2, 8, 128), jnp.int32),
             pltpu.SMEM((2, 2, 8, 128), jnp.int32),
-            dma((NB,)), dma((2, ROWS)), dma((NB,)), dma((NB, 2)), dma((2, ROWS, 2)),
+            dma((NB,)), dma((2, ROWS)), dma((NB,)), dma((NB, 2)), dma((2, ROWS, 2)), dma((2,)), dma((2,)),
             dma((2, 2, CH, 8)), dma((CH, NONE)), dma((2, ROWS)), dma((NB,)),
-            dma((CH, 2, 3)), dma((CH, 2, 3)), dma((CH, 2, 3)), dma((CH, 2, 3)),
-            dma((CH,)), dma((CH, 2)), dma((2,)), dma, dma,
+            dma((CH, 2, 3)), dma((CH, 2, 3)), dma((CH, 2, 4, 2)), dma((CH, 2, 4, 2)),
+            dma((CH, 2)), dma((2,)), dma, dma, pltpu.SemaphoreType.REGULAR,
+            *[pltpu.VMEM((NONE + 1, CR, FW), BF16)] * CH,
         ],
         compiler_params=pltpu.CompilerParams(
             collective_id=0, has_side_effects=True, vmem_limit_bytes=58 * 2**20

time: 177 us -> 150 us (0.85)
  Pallas kernels: 171 us -> 146 us
    pallas_call x1, Pallas kernels: 171 us -> 146 us  [per_device(): pl.pallas_call(kernel, out_shape=(jax.ShapeDtypeStruct((NB, QF, FW), BF16...]
where the time goes in v3:
time: 150 us
  Pallas kernels  146 us (97%)
  local copies, waits for them, and re-layouts  3.34 us (2%)
    pallas_call x1, Pallas kernels, per_device(): pl.pallas_call(kernel, out_shape=(jax.ShapeDtypeStruct((NB, QF, FW), BF16...  146 us
    unnamed x4, local copies, waits for them, and re-layouts  3.34 us

profile of v3, /device:TPU:1, one launch (start us, length us, event | category | flops | bytes accessed | tf_op | source)
XLA Modules:
  0.0 149.6 jit_solution(9130818660141005879)
XLA Ops:
  0.6 145.6 %condense.1 = (bf16[5,192,768]{2,1,0:T(8,128)(2,1)}, bf16[1,192,768]{2,1,0:T(8,128)(2,1)}) custom-call(bf16[5,256,1024]{2,1,0:T(8,128)(2,1)} %stiff.1, bf16[5,256,2,768]{3,2,1,0:T(2,128)(2,1)} %coup.1, f32[5,256]{1,0:T(8,128)} %scale.1, s32[2,5]{1,0:T(2,128)} %bitcast.1), custom_call_target="tpu_custom_call" | custom-call | flops 8556380160 | bytes 9437184 | tf_op jit(solution)/shard_map/condense/pallas_call | solution.py:452
  146.3 0.0 copy-start
  146.3 2.6 %copy.8 = bf16[5,192,768]{2,1,0:T(8,128)(2,1)} copy(bf16[5,192,768]{2,1,0:T(8,128)(2,1)} %get-tuple-element.4) | data formatting | bytes 2949120
  148.9 0.0 copy-done
  148.9 0.7 copy.9
Async XLA Ops:
  146.3 2.6 %copy-start = (bf16[1,192,768]{2,1,0:T(8,128)(2,1)S(1)}, bf16[1,192,768]{2,1,0:T(8,128)(2,1)}, u32[]{:S(2)}) copy-start(bf16[1,192,768]{2,1,0:T(8,128)(2,1)} %get-tuple-element.5) | copy-start | bytes 884740

commit v4 on v3

--- a/solution.py
+++ b/solution.py
@@ -19,7 +19,7 @@
 HF = QF // 2
 HC = FW // 2
 NONE = 4 * NB
-CH = 3
+CH = 6
 CR = HF // CH
 
 
@@ -59,15 +59,6 @@
     for load in loads:
         load.start()
 
-    lane = lax.broadcasted_iota(jnp.int32, (8, 128), 1)
-    low, high = jnp.full((8, 128), NONE, jnp.int32), jnp.full((8, 128), -1, jnp.int32)
-    for e in range(2 * NB):
-        hit = lane == jnp.broadcast_to(masters[pl.ds(e % 2, 1), pl.ds(e // 2, 1)], (8, 128))
-        low = jnp.minimum(low, jnp.where(hit, core * 2 * NB + e, NONE))
-        high = jnp.maximum(high, jnp.where(hit, core * 2 * NB + e, -1))
-    own_table[0] = low
-    own_table[1] = jnp.where(high > low, high, NONE)
-
     barrier = pltpu.get_barrier_semaphore()
     partners = [(r, other)]
     for d in (1, 2, 3):
@@ -77,38 +68,45 @@
             partners += [(r, at_y(lax.rem(y + d, 4), h)), (r, at_z(lax.rem(z + d, 4), h))]
     for device in partners:
         pl.semaphore_signal(barrier, inc=1, device_id=device, device_id_type=MESH)
-    pl.semaphore_wait(barrier, len(partners))
+    lane = lax.broadcasted_iota(jnp.int32, (8, 128), 1)
+    low, high = jnp.full((8, 128), NONE, jnp.int32), jnp.full((8, 128), -1, jnp.int32)
+    for e in range(2 * NB):
+        hit = lane == jnp.broadcast_to(masters[pl.ds(e % 2, 1), pl.ds(e // 2, 1)], (8, 128))
+        low = jnp.minimum(low, jnp.where(hit, core * 2 * NB + e, NONE))
+        high = jnp.maximum(high, jnp.where(hit, core * 2 * NB + e, -1))
+    own_table[0] = low
+    own_table[1] = jnp.where(high > low, high, NONE)
 
     mine = pl.ds(pl.multiple_of(r * QN, QN), QN)
 
-    def k_copy(i, b, slot, row):
-        return remote(stiff.at[b], kbuf.at[slot, mine], k_send.at[i], k_recv.at[slot, r], (row, c))
+    def k_copy(b, slot, row):
+        return remote(stiff.at[b], kbuf.at[slot, mine], k_send.at[slot], k_recv.at[slot], (row, c))
 
     def k_local(b, slot):
-        return pltpu.make_async_copy(stiff.at[b], kbuf.at[slot, mine], k_recv.at[slot, r])
-
-    def p_copy(i, b, slot, row, k):
+        return pltpu.make_async_copy(stiff.at[b], kbuf.at[slot, mine], k_recv.at[slot])
+
+    def p_copy(b, slot, row, k):
         return remote(
             ploc.at[b, pl.ds(k * FW, FW)], pbuf.at[slot, pl.ds(k * FW, FW), mine],
-            p_send.at[i, k], p_recv.at[slot, r, k], (row, c),
+            p_send.at[slot], p_recv.at[slot, k], (row, c),
         )
 
     def p_aside(k):
         return remote(
             ploc.at[4, pl.ds(k * FW, FW)], relay.at[pl.ds(k * FW, FW)],
-            p_send.at[0, k], r_recv.at[k], (through, c),
+            p_send.at[0], r_recv.at[k], (through, c),
         )
 
     def p_forward(k):
         return remote(
             relay.at[pl.ds(k * FW, FW)],
             pbuf.at[0, pl.ds(k * FW, FW), pl.ds(pl.multiple_of(far * QN, QN), QN)],
-            r_send.at[k], p_recv.at[0, far, k], (target, c),
+            r_send, p_recv.at[0, k], (target, c),
         )
 
     def p_local(b, slot, k):
         return pltpu.make_async_copy(
-            ploc.at[b, pl.ds(k * FW, FW)], pbuf.at[slot, pl.ds(k * FW, FW), mine], p_recv.at[slot, r, k]
+            ploc.at[b, pl.ds(k * FW, FW)], pbuf.at[slot, pl.ds(k * FW, FW), mine], p_recv.at[slot, k]
         )
 
     def send_block(i, remote_copy, local_copy, aside=None):
@@ -119,7 +117,7 @@
 
             @pl.when((r != target) & (r != far if aside else True))
             def _():
-                remote_copy(0, 4, 0, target).start()
+                remote_copy(4, 0, target).start()
 
             if aside:
                 @pl.when(r == far)
@@ -128,13 +126,11 @@
         elif i == 3:
             @pl.when(r != through)
             def _():
-                remote_copy(i, order[i], 1, order[i]).start()
+                remote_copy(order[i], 1, order[i]).start()
         elif i < 4:
-            remote_copy(i, order[i], 1, order[i]).start()
+            remote_copy(order[i], 1, order[i]).start()
         else:
             local_copy(order[i], 1).start()
-
-    send_block(0, k_copy, k_local)
 
     def project(i, k):
         b = order[i]
@@ -142,17 +138,24 @@
             loads[i].wait()
         raw = cin[b, :, k, :].astype(F32).T
         ploc[b, pl.ds(k * FW, FW), :] = (raw / scale[pl.ds(b, 1), :]).astype(BF16)
+
+    def p_start(i, k):
         send_block(
             i, functools.partial(p_copy, k=k), functools.partial(p_local, k=k), functools.partial(p_aside, k)
         )
 
     project(0, 0)
     project(0, 1)
+    pl.semaphore_wait(barrier, len(partners))
+    send_block(0, k_copy, k_local)
+    p_start(0, 0)
+    p_start(0, 1)
     for i in range(1, NB):
         send_block(i, k_copy, k_local)
     for k in range(2):
         for i in range(1, NB):
             project(i, k)
+            p_start(i, k)
 
     own_idx = pltpu.make_async_copy(own_table, idx_v.at[core], i_sem.at[0])
     own_idx.start()
@@ -172,11 +175,11 @@
         for k in range(2):
             wait(relay.at[pl.ds(k * FW, FW)], r_recv.at[k])
             p_forward(k).start()
-        k_copy(3, order[3], 1, order[3]).start()
+        k_copy(order[3], 1, order[3]).start()
         for k in range(2):
-            p_copy(3, order[3], 1, order[3], k).start()
-
-    def t_copies(slot, b, f, j, local=True):
+            p_copy(order[3], 1, order[3], k).start()
+
+    def t_copies(slot, b, f, j):
         at = core * 2 * NB + b * 2 + f
         copies = []
         for dq in range(ROWS):
@@ -186,21 +189,21 @@
                 dst = terms[j].at[at]
                 if dq or dh:
                     copies.append(remote(
-                        src, dst, t_send.at[slot, f, j, dq * 2 + dh], t_recv.at[j, at], (q, c - core + h)
+                        src, dst, t_send.at[slot, j], t_recv.at[j], (q, c - core + h)
                     ))
-                elif local:
-                    copies.append(pltpu.make_async_copy(src, dst, t_recv.at[j, at]))
+                else:
+                    copies.append(pltpu.make_async_copy(src, dst, t_recv.at[j]))
         return copies
 
-    def x_copies(slot, b, local=True):
+    def x_copies(slot, b):
         copies = []
         for dq in range(ROWS):
             q = lax.rem(r + dq, ROWS)
             src = fills.at[slot, 2, pl.ds(pl.multiple_of(q * QF, QF), QF)]
             if dq:
-                copies.append(remote(src, cross.at[b], x_send.at[slot, dq], x_recv.at[b], (q, c)))
-            elif local:
-                copies.append(pltpu.make_async_copy(src, cross.at[b], x_recv.at[b]))
+                copies.append(remote(src, cross.at[b], x_send.at[slot], x_recv, (q, c)))
+            else:
+                copies.append(pltpu.make_async_copy(src, cross.at[b], x_recv))
         return copies
 
     def fill(slot, f, a, b):
@@ -223,16 +226,14 @@
         b = jnp.where(slot == 0, 4, r)
 
         def p_wait(k):
-            for j in range(ROWS):
-                wait(pbuf.at[slot, pl.ds(k * FW, FW), pl.ds(j * QN, QN)], p_recv.at[slot, j, k])
+            wait(pbuf.at[slot, pl.ds(k * FW, FW)], p_recv.at[slot, k])
 
         def t_start(f, j):
             for copy in t_copies(slot, b, f, j):
                 copy.start()
 
         def k_wait():
-            for j in range(ROWS):
-                wait(kbuf.at[slot, pl.ds(j * QN, QN)], k_recv.at[slot, j])
+            wait(kbuf.at[slot], k_recv.at[slot])
 
         k_wait()
         p_wait(0)
@@ -271,35 +272,21 @@
 
     owner = r == target
     def k_drain():
+        wait(kbuf.at[1, pl.ds(0, 3 * QN)], k_send.at[1])
+        wait(pbuf.at[1, pl.ds(0, 3 * FW // 2)], p_send.at[1])
+
         @pl.when(r != target)
         def _():
-            k_copy(0, 4, 0, target).wait_send()
-
-        @pl.when((r != target) & (r != far))
-        def _():
-            for k in range(2):
-                p_copy(0, 4, 0, target, k).wait_send()
-
-        @pl.when(r == far)
-        def _():
-            for k in range(2):
-                p_aside(k).wait_send()
+            wait(kbuf.at[1, pl.ds(0, QN)], k_send.at[0])
+            wait(ploc.at[4], p_send.at[0])
 
         @pl.when(r == through)
         def _():
-            for k in range(2):
-                p_forward(k).wait_send()
-
-        for i in (1, 2, 3):
-            k_copy(i, order[i], 1, order[i]).wait_send()
-            for k in range(2):
-                p_copy(i, order[i], 1, order[i], k).wait_send()
+            wait(relay, r_send)
 
     def t_drain(j):
         def one(slot, unused):
-            for f in range(2):
-                for copy in t_copies(slot, jnp.where(slot == 0, 4, r), f, j, False):
-                    copy.wait_send()
+            wait(terms[j].at[pl.ds(0, 14)], t_send.at[slot, j])
             return unused
 
         lax.fori_loop(first_slot, 2, one, 0)
@@ -341,7 +328,7 @@
         lead = lax.rem(place[half] + d, 4)
         return remote(
             dense.at[j, half, lead], got1.at[j, half, d - 1],
-            s1_send.at[j, half, d - 1], s1_recv.at[j, half, d - 1], (r, whom[half](lead)),
+            s1_send.at[j], s1_recv.at[j], (r, whom[half](lead)),
         )
 
     def second_copies(j, half, d):
@@ -349,23 +336,19 @@
         return [
             remote(
                 part.at[j, half, o, h], got2.at[j, half, d, core],
-                s2_send.at[j, half, d, e], s2_recv.at[j, half, d, core], (r, whom[1 - half](o, h)),
+                s2_send.at[j], s2_recv.at[j], (r, whom[1 - half](o, h)),
             )
-            for e, h in ((0, core), (1, 1 - core)) if d or e
+            for h in (core, 1 - core)[0 if d else 1:]
         ]
 
     def t_wait(j):
-        for at in range(NONE):
-            wait(terms[j].at[at], t_recv.at[j, at])
-
-    def first_wait(j, half):
-        for d in (1, 2, 3):
-            first_copy(j, half, d).wait_recv()
-
-    def second_wait(j, half):
-        for d in range(4):
-            for h in (1 - core, core) if d else (1 - core,):
-                wait(got2.at[j, half, d, h], s2_recv.at[j, half, d, h])
+        wait(terms[j].at[pl.ds(0, NONE)], t_recv.at[j])
+
+    def first_wait(j):
+        wait(got1.at[j], s1_recv.at[j])
+
+    def second_wait(j):
+        wait(got2.at[j], s2_recv.at[j])
 
     def stage0(j):
         t_wait(j)
@@ -377,8 +360,8 @@
 
     def stage1(j):
         t_drain(j)
+        first_wait(j)
         for half in range(2):
-            first_wait(j, half)
             for d in (2, 1, 3, 0):
                 o = lax.rem(place[1 - half] + d, 4)
                 total = dense[j, half, place[half], o].astype(F32)
@@ -387,22 +370,23 @@
                 part[j, half, o] = total.astype(BF16)
                 for copy in second_copies(j, half, d):
                     copy.start()
-            got2[j, half, 0, core] = part[j, half, place[1 - half], core]
+            pltpu.make_async_copy(
+                part.at[j, half, place[1 - half], core], got2.at[j, half, 0, core], s2_recv.at[j]
+            ).start()
 
     def out_copy(j, h):
         rows = pl.ds(h * HF + j * CR, CR)
-        return pltpu.make_async_copy(last.at[rows], diag.at[0, rows], f_sem.at[j, h])
+        return pltpu.make_async_copy(last.at[rows], diag.at[0, rows], f_sem)
+
+    def second_drain(j):
+        wait(terms[j].at[pl.ds(0, 7)], s2_send.at[j])
 
     def stage2(j):
+        wait(got1.at[j], s1_send.at[j])
+        if j:
+            second_drain(j - 1)
+        second_wait(j)
         for half in range(2):
-            for d in (1, 2, 3):
-                first_copy(j, half, d).wait_send()
-            if j:
-                for d in range(4):
-                    for copy in second_copies(j - 1, half, d):
-                        copy.wait_send()
-        for half in range(2):
-            second_wait(j, half)
             total = got2[j, half, 0].astype(F32)
             for d in (1, 2, 3):
                 total += got2[j, half, d].astype(F32)
@@ -424,24 +408,17 @@
     stage2(CH - 1)
 
     def x_wait():
-        for b in range(NB):
-            wait(cross.at[b], x_recv.at[b])
+        wait(cross, x_recv)
 
     x_wait()
-    for j in range(CH):
-        for h in range(2):
-            out_copy(j, h).wait()
-    for d in range(4):
-        for half in range(2):
-            for copy in second_copies(CH - 1, half, d):
-                copy.wait_send()
-
-    def x_drain(slot, unused):
-        for copy in x_copies(slot, jnp.where(slot == 0, 4, r), False):
-            copy.wait_send()
-        return unused
-
-    lax.fori_loop(first_slot, 2, x_drain, 0)
+    second_drain(CH - 1)
+    wait(cross.at[pl.ds(0, 3)], x_send.at[1])
+
+    @pl.when(owner)
+    def _():
+        wait(cross.at[pl.ds(0, 3)], x_send.at[0])
+
+    wait(diag, f_sem)
 
 
 def per_device(stiffness, coupling, slave_diag, slave_masters):
@@ -473,10 +450,9 @@
             pltpu.VMEM((2, 8, 128), jnp.int32),
             pltpu.VMEM((2, 2, 8, 128), jnp.int32),
             pltpu.SMEM((2, 2, 8, 128), jnp.int32),
-            dma((NB,)), dma((2, ROWS)), dma((NB,)), dma((NB, 2)), dma((2, ROWS, 2)), dma((2,)), dma((2,)),
-            dma((2, 2, CH, 8)), dma((CH, NONE)), dma((2, ROWS)), dma((NB,)),
-            dma((CH, 2, 3)), dma((CH, 2, 3)), dma((CH, 2, 4, 2)), dma((CH, 2, 4, 2)),
-            dma((CH, 2)), dma((2,)), dma, dma, pltpu.SemaphoreType.REGULAR,
+            dma((2,)), dma((2,)), dma((NB,)), dma((2,)), dma((2, 2)), dma, dma((2,)),
+            dma((2, CH)), dma((CH,)), dma((2,)), dma,
+            dma((CH,)), dma((CH,)), dma((CH,)), dma((CH,)), dma, dma((2,)), dma, dma, pltpu.SemaphoreType.REGULAR,
             *[pltpu.VMEM((NONE + 1, CR, FW), BF16)] * CH,
         ],
         compiler_params=pltpu.CompilerParams(

time: 150 us -> 143 us (0.953)
  Pallas kernels: 146 us -> 139 us
    pallas_call x1, Pallas kernels: 146 us -> 139 us  [per_device(): pl.pallas_call(kernel, out_shape=(jax.ShapeDtypeStruct((NB, QF, FW), BF16...]
where the time goes in v4:
time: 143 us
  Pallas kernels  139 us (97%)
  local copies, waits for them, and re-layouts  3.34 us (2%)
    pallas_call x1, Pallas kernels, per_device(): pl.pallas_call(kernel, out_shape=(jax.ShapeDtypeStruct((NB, QF, FW), BF16...  139 us
    unnamed x4, local copies, waits for them, and re-layouts  3.34 us

profile of v4, /device:TPU:1, one launch (start us, length us, event | category | flops | bytes accessed | tf_op | source)
XLA Modules:
  0.0 143.0 jit_solution(6683083331487256995)
XLA Ops:
  0.6 139.0 %condense.1 = (bf16[5,192,768]{2,1,0:T(8,128)(2,1)}, bf16[1,192,768]{2,1,0:T(8,128)(2,1)}) custom-call(bf16[5,256,1024]{2,1,0:T(8,128)(2,1)} %stiff.1, bf16[5,256,2,768]{3,2,1,0:T(2,128)(2,1)} %coup.1, f32[5,256]{1,0:T(8,128)} %scale.1, s32[2,5]{1,0:T(2,128)} %bitcast.1), custom_call_target="tpu_custom_call" | custom-call | flops 8556380160 | bytes 9437184 | tf_op jit(solution)/shard_map/condense/pallas_call | solution.py:429
  139.7 0.0 copy-start
  139.7 2.6 %copy.8 = bf16[5,192,768]{2,1,0:T(8,128)(2,1)} copy(bf16[5,192,768]{2,1,0:T(8,128)(2,1)} %get-tuple-element.4) | data formatting | bytes 2949120
  142.3 0.0 copy-done
  142.3 0.7 copy.9
Async XLA Ops:
  139.7 2.6 %copy-start = (bf16[1,192,768]{2,1,0:T(8,128)(2,1)S(1)}, bf16[1,192,768]{2,1,0:T(8,128)(2,1)}, u32[]{:S(2)}) copy-start(bf16[1,192,768]{2,1,0:T(8,128)(2,1)} %get-tuple-element.5) | copy-start | bytes 884740

commit v5 on v4

--- a/solution.py
+++ b/solution.py
@@ -26,8 +26,8 @@
 def kernel(
     stiff, coup, scale, masters,
     cross, diag,
-    kbuf, pbuf, cin, ploc, relay, left, fills, dense, got1, part, got2, last, own_table, idx_v, idx_s,
-    k_send, k_recv, c_sem, p_send, p_recv, r_send, r_recv, t_send, t_recv, x_send, x_recv,
+    kbuf, pbuf, cin, ploc, relay, x_relay, left, fills, dense, got1, part, got2, last, own_table, idx_v, idx_s,
+    k_send, k_recv, c_sem, p_send, p_recv, r_send, r_recv, t_send, t_recv, x_send, x_recv, xr_send, xr_recv,
     s1_send, s1_recv, s2_send, s2_recv, f_sem, i_sem, i_send, i_recv, ready, *terms,
 ):
     r = lax.axis_index("row")
@@ -39,6 +39,7 @@
     target = 2 * core
     through = target + 1
     far = lax.rem(target + 2, ROWS)
+    back = lax.rem(target + 3, ROWS)
 
     def at_y(v, h=core):
         return z * 8 + v * 2 + h
@@ -195,9 +196,18 @@
                     copies.append(pltpu.make_async_copy(src, dst, t_recv.at[j]))
         return copies
 
+    def x_aside():
+        src = fills.at[0, 2, pl.ds(pl.multiple_of(far * QF, QF), QF)]
+        return remote(src, x_relay, x_send.at[0], xr_recv, (back, c))
+
+    def x_forward():
+        return remote(x_relay, cross.at[4], xr_send, x_recv, (far, c))
+
     def x_copies(slot, b):
         copies = []
         for dq in range(ROWS):
+            if slot == 0 and dq == 2:
+                continue
             q = lax.rem(r + dq, ROWS)
             src = fills.at[slot, 2, pl.ds(pl.multiple_of(q * QF, QF), QF)]
             if dq:
@@ -206,13 +216,26 @@
                 copies.append(pltpu.make_async_copy(src, cross.at[b], x_recv))
         return copies
 
-    def fill(slot, f, a, b):
+    def fill(slot, f, a, b, skip=False):
         for n in range(3):
             out = lax.dot_general(
                 left[a], pbuf[slot, pl.ds(b * FW + n * 256, 256), :],
                 (((1,), (1,)), ((), ())), preferred_element_type=F32,
-            )
-            fills[slot, f, :, pl.ds(n * 256, 256)] = out.astype(BF16)
+            ).astype(BF16)
+            if skip:
+                for q in range(2 * ROWS):
+                    fills[slot, f, pl.ds(q * HF + CR, HF - CR), pl.ds(n * 256, 256)] = out[q * HF + CR:(q + 1) * HF]
+            else:
+                fills[slot, f, :, pl.ds(n * 256, 256)] = out
+
+    def fill_head(f):
+        rows = [pbuf[1, pl.ds(f * FW + q * HF, CR), :] for q in range(2 * ROWS)]
+        head = jnp.dot(jnp.concatenate(rows), kbuf[1], preferred_element_type=F32).astype(BF16)
+        out = lax.dot_general(
+            head, pbuf[1, pl.ds(f * FW, FW), :], (((1,), (1,)), ((), ())), preferred_element_type=F32
+        ).astype(BF16)
+        for q in range(2 * ROWS):
+            fills[1, f, pl.ds(q * HF, CR), :] = out[q * CR:(q + 1) * CR]
 
     def multiply(slot, k):
         for n in range(4):
@@ -235,31 +258,44 @@
         def k_wait():
             wait(kbuf.at[slot], k_recv.at[slot])
 
+        def tell(stage):
+            for device in ring:
+                pl.semaphore_signal(ready.at[stage], inc=1, device_id=device, device_id_type=MESH)
+
         k_wait()
         p_wait(0)
         multiply(slot, 0)
         fill(slot, 0, 0, 0)
-        p_wait(1)
 
         @pl.when(owner & (slot == 1))
         def _():
-            for device in ring:
-                pl.semaphore_signal(ready, inc=1, device_id=device, device_id_type=MESH)
+            tell(0)
             t_start(0, 0)
-
-        multiply(slot, 1)
-        fill(slot, 1, 1, 1)
-
-        @pl.when(jnp.logical_not(owner))
-        def _():
-            fill(slot, 2, 0, 1)
-            pl.semaphore_wait(ready, 2)
+            p_wait(1)
+            tell(1)
+            fill_head(1)
+            t_start(1, 0)
+            multiply(slot, 1)
+            fill(slot, 1, 1, 1, skip=True)
 
         @pl.when(jnp.logical_not(owner & (slot == 1)))
         def _():
+            p_wait(1)
+            multiply(slot, 1)
+            fill(slot, 1, 1, 1)
+
+            @pl.when(jnp.logical_not(owner))
+            def _():
+                fill(slot, 2, 0, 1)
+                pl.semaphore_wait(ready.at[0], 2)
+
             t_start(0, 0)
-
-        t_start(1, 0)
+            t_start(1, 0)
+
+            @pl.when(jnp.logical_not(owner))
+            def _():
+                pl.semaphore_wait(ready.at[1], 2)
+
         for j in range(1, CH):
             for f in range(2):
                 t_start(f, j)
@@ -267,6 +303,10 @@
         @pl.when(owner)
         def _():
             fill(slot, 2, 0, 1)
+
+        @pl.when(slot == 0)
+        def _():
+            x_aside().start()
 
         return unused
 
@@ -301,7 +341,13 @@
     def _():
         for copy in x_copies(0, 4):
             copy.start()
-        pl.semaphore_wait(ready, 1)
+        for stage in range(2):
+            pl.semaphore_wait(ready.at[stage], 1)
+
+    @pl.when(r == back)
+    def _():
+        wait(x_relay, xr_recv)
+        x_forward().start()
 
     k_drain()
 
@@ -418,6 +464,10 @@
     def _():
         wait(cross.at[pl.ds(0, 3)], x_send.at[0])
 
+    @pl.when(r == back)
+    def _():
+        wait(x_relay, xr_send)
+
     wait(diag, f_sem)
 
 
@@ -428,18 +478,16 @@
     flops = 2 * NB * (2 * NS * NS * FW + 3 * FW * FW * NS) // 4
     return pl.pallas_call(
         kernel,
-        out_shape=(
-            jax.ShapeDtypeStruct((NB, QF, FW), BF16),
-            jax.ShapeDtypeStruct((1, QF, FW), BF16),
-        ),
+        out_shape=(pltpu.VMEM((NB, QF, FW), BF16), pltpu.VMEM((1, QF, FW), BF16)),
         in_specs=[any_space, any_space, vmem, vmem],
-        out_specs=(any_space, any_space),
+        out_specs=(vmem, vmem),
         scratch_shapes=[
             pltpu.VMEM((2, NS, NS), BF16),
             pltpu.VMEM((2, 2 * FW, NS), BF16),
             pltpu.VMEM((NB, QN, 2, FW), BF16),
             pltpu.VMEM((NB, 2 * FW, QN), BF16),
             pltpu.VMEM((2 * FW, QN), BF16),
+            pltpu.VMEM((QF, FW), BF16),
             pltpu.VMEM((2, FW, NS), BF16),
             pltpu.VMEM((2, 3, FW, FW), BF16),
             pltpu.VMEM((CH, 2, 4, 4, 2, CR, HC), BF16),
@@ -451,8 +499,8 @@
             pltpu.VMEM((2, 2, 8, 128), jnp.int32),
             pltpu.SMEM((2, 2, 8, 128), jnp.int32),
             dma((2,)), dma((2,)), dma((NB,)), dma((2,)), dma((2, 2)), dma, dma((2,)),
-            dma((2, CH)), dma((CH,)), dma((2,)), dma,
-            dma((CH,)), dma((CH,)), dma((CH,)), dma((CH,)), dma, dma((2,)), dma, dma, pltpu.SemaphoreType.REGULAR,
+            dma((2, CH)), dma((CH,)), dma((2,)), dma, dma, dma,
+            dma((CH,)), dma((CH,)), dma((CH,)), dma((CH,)), dma, dma((2,)), dma, dma, pltpu.SemaphoreType.REGULAR((2,)),
             *[pltpu.VMEM((NONE + 1, CR, FW), BF16)] * CH,
         ],
         compiler_params=pltpu.CompilerParams(

time: 143 us -> 139 us (0.972)
  Pallas kernels: 139 us -> 136 us
  local copies, waits for them, and re-layouts: 3.34 us -> 1.83 us
    pallas_call x1, Pallas kernels: 139 us -> 136 us  [per_device(): pl.pallas_call(kernel, out_shape=(pltpu.VMEM((NB, QF, FW), BF16), pltpu.V...]
    unnamed x4 -> x2, local copies, waits for them, and re-layouts: 3.34 us -> 1.83 us
where the time goes in v5:
time: 139 us
  Pallas kernels  136 us (98%)
  local copies, waits for them, and re-layouts  1.83 us (1%)
    pallas_call x1, Pallas kernels, per_device(): pl.pallas_call(kernel, out_shape=(pltpu.VMEM((NB, QF, FW), BF16), pltpu.V...  136 us

profile of v5, /device:TPU:1, one launch (start us, length us, event | category | flops | bytes accessed | tf_op | source)
XLA Modules:
  0.0 138.8 jit_solution(11044436212201246821)
XLA Ops:
  0.6 136.3 %condense.1 = (bf16[5,192,768]{2,1,0:T(8,128)(2,1)S(1)}, bf16[1,192,768]{2,1,0:T(8,128)(2,1)S(1)}) custom-call(bf16[5,256,1024]{2,1,0:T(8,128)(2,1)} %stiff.1, bf16[5,256,2,768]{3,2,1,0:T(2,128)(2,1)} %coup.1, f32[5,256]{1,0:T(8,128)} %scale.1, s32[2,5]{1,0:T(2,128)} %bitcast.1), custom_call_target="tpu_custom_call" | custom-call | flops 8556380160 | bytes 9437184 | tf_op jit(solution)/shard_map/condense/pallas_call | solution.py:479
  136.9 1.1 copy.8
  138.1 0.7 copy.9

commit v6 on v5

--- a/solution.py
+++ b/solution.py
@@ -21,14 +21,16 @@
 NONE = 4 * NB
 CH = 6
 CR = HF // CH
+X_AT = 4
 
 
 def kernel(
-    stiff, coup, scale, masters,
+    stiff, coup, scale_in, masters_in,
     cross, diag,
-    kbuf, pbuf, cin, ploc, relay, x_relay, left, fills, dense, got1, part, got2, last, own_table, idx_v, idx_s,
+    kbuf, pbuf, cin, scale, masters, ploc, relay, x_relay, left, fills, dense, hop, got1, part, got2,
+    own_table, idx_v, idx_s,
     k_send, k_recv, c_sem, p_send, p_recv, r_send, r_recv, t_send, t_recv, x_send, x_recv, xr_send, xr_recv,
-    s1_send, s1_recv, s2_send, s2_recv, f_sem, i_sem, i_send, i_recv, ready, *terms,
+    s1_send, s1_recv, s2_send, s2_recv, h_recv, b_send, i_sem, i_send, i_recv, small, ready, *terms,
 ):
     r = lax.axis_index("row")
     c = lax.axis_index("col")
@@ -55,11 +57,6 @@
             src_ref=src, dst_ref=dst, send_sem=send, recv_sem=recv, device_id=device, device_id_type=MESH
         )
 
-    order = [4] + [lax.rem(r + d, ROWS) for d in (1, 2, 3, 0)]
-    loads = [pltpu.make_async_copy(coup.at[b], cin.at[b], c_sem.at[i]) for i, b in enumerate(order)]
-    for load in loads:
-        load.start()
-
     barrier = pltpu.get_barrier_semaphore()
     partners = [(r, other)]
     for d in (1, 2, 3):
@@ -69,14 +66,26 @@
             partners += [(r, at_y(lax.rem(y + d, 4), h)), (r, at_z(lax.rem(z + d, 4), h))]
     for device in partners:
         pl.semaphore_signal(barrier, inc=1, device_id=device, device_id_type=MESH)
+    order = [4] + [lax.rem(r + d, ROWS) for d in (1, 2, 3, 0)]
+    loads = [pltpu.make_async_copy(coup.at[b], cin.at[b], c_sem.at[i]) for i, b in enumerate(order)]
+    for load in loads:
+        load.start()
+    small_loads = [
+        pltpu.make_async_copy(scale_in, scale, small.at[0]), pltpu.make_async_copy(masters_in, masters, small.at[1])
+    ]
+    for load in small_loads:
+        load.start()
+
+    for load in small_loads:
+        load.wait()
     lane = lax.broadcasted_iota(jnp.int32, (8, 128), 1)
-    low, high = jnp.full((8, 128), NONE, jnp.int32), jnp.full((8, 128), -1, jnp.int32)
+    least, most = jnp.full((8, 128), NONE, jnp.int32), jnp.full((8, 128), -1, jnp.int32)
     for e in range(2 * NB):
         hit = lane == jnp.broadcast_to(masters[pl.ds(e % 2, 1), pl.ds(e // 2, 1)], (8, 128))
-        low = jnp.minimum(low, jnp.where(hit, core * 2 * NB + e, NONE))
-        high = jnp.maximum(high, jnp.where(hit, core * 2 * NB + e, -1))
-    own_table[0] = low
-    own_table[1] = jnp.where(high > low, high, NONE)
+        least = jnp.minimum(least, jnp.where(hit, core * 2 * NB + e, NONE))
+        most = jnp.maximum(most, jnp.where(hit, core * 2 * NB + e, -1))
+    own_table[0] = least
+    own_table[1] = jnp.where(most > least, most, NONE)
 
     mine = pl.ds(pl.multiple_of(r * QN, QN), QN)
 
@@ -334,20 +343,25 @@
     first_slot = jnp.where(owner, 0, 1)
     ring = [(r, other)] + [(lax.rem(r + d, ROWS), col) for d in (1, 2, 3) for col in (c, other)]
     lax.fori_loop(first_slot, 2, block, 0)
-    for copy in x_copies(1, r):
-        copy.start()
-
-    @pl.when(r == target)
+
+    @pl.when(owner)
     def _():
-        for copy in x_copies(0, 4):
-            copy.start()
         for stage in range(2):
             pl.semaphore_wait(ready.at[stage], 1)
 
-    @pl.when(r == back)
-    def _():
-        wait(x_relay, xr_recv)
-        x_forward().start()
+    def x_start():
+        for copy in x_copies(1, r):
+            copy.start()
+
+        @pl.when(owner)
+        def _():
+            for copy in x_copies(0, 4):
+                copy.start()
+
+        @pl.when(r == back)
+        def _():
+            wait(x_relay, xr_recv)
+            x_forward().start()
 
     k_drain()
 
@@ -370,12 +384,40 @@
 
         lax.fori_loop(0, 8, one, 0)
 
-    def first_copy(j, half, d):
-        lead = lax.rem(place[half] + d, 4)
+    after, before, low, high = 1, 3, pl.ds(0, 2), pl.ds(2, 2)
+
+    def lead_of(half, d):
+        return lax.rem(place[half] + d, 4)
+
+    def ring_copy(j, half, lead, part_of, dst, send, recv, d):
         return remote(
-            dense.at[j, half, lead], got1.at[j, half, d - 1],
-            s1_send.at[j], s1_recv.at[j], (r, whom[half](lead)),
-        )
+            dense.at[j, half, lead_of(half, lead), part_of], dst, send.at[j], recv.at[j],
+            (r, whom[half](lead_of(half, d))),
+        )
+
+    def first_copies(j, half, d):
+        if d == 2:
+            return [
+                ring_copy(j, half, 2, low, hop.at[j, half, 0], s1_send, h_recv, after),
+                ring_copy(j, half, 2, high, hop.at[j, half, 1], s1_send, h_recv, before),
+            ]
+        if d == after:
+            return [ring_copy(j, half, d, high, got1.at[j, half, 0, high], s1_send, s1_recv, d)]
+        if d == before:
+            return [ring_copy(j, half, d, low, got1.at[j, half, 1, low], s1_send, s1_recv, d)]
+        return []
+
+    def hop_wait(j):
+        wait(hop.at[j], h_recv.at[j])
+
+    def stage_hop(j):
+        hop_wait(j)
+        for half in range(2):
+            for n, d, part_of in ((0, after, low), (1, before, high)):
+                lead = lead_of(half, d)
+                total = dense[j, half, lead, part_of].astype(F32) + hop[j, half, n].astype(F32)
+                dense[j, half, lead, part_of] = total.astype(BF16)
+                ring_copy(j, half, d, part_of, got1.at[j, half, n, part_of], b_send, s1_recv, d).start()
 
     def second_copies(j, half, d):
         o = lax.rem(place[1 - half] + d, 4)
@@ -401,8 +443,8 @@
         for d in (2, 1, 3, 0):
             for half in range(2):
                 sum_terms(j, half, lax.rem(place[half] + d, 4))
-                if d:
-                    first_copy(j, half, d).start()
+                for copy in first_copies(j, half, d):
+                    copy.start()
 
     def stage1(j):
         t_drain(j)
@@ -411,7 +453,7 @@
             for d in (2, 1, 3, 0):
                 o = lax.rem(place[1 - half] + d, 4)
                 total = dense[j, half, place[half], o].astype(F32)
-                for e in range(3):
+                for e in range(2):
                     total += got1[j, half, e, o].astype(F32)
                 part[j, half, o] = total.astype(BF16)
                 for copy in second_copies(j, half, d):
@@ -420,15 +462,12 @@
                 part.at[j, half, place[1 - half], core], got2.at[j, half, 0, core], s2_recv.at[j]
             ).start()
 
-    def out_copy(j, h):
-        rows = pl.ds(h * HF + j * CR, CR)
-        return pltpu.make_async_copy(last.at[rows], diag.at[0, rows], f_sem)
-
     def second_drain(j):
         wait(terms[j].at[pl.ds(0, 7)], s2_send.at[j])
 
     def stage2(j):
         wait(got1.at[j], s1_send.at[j])
+        wait(hop.at[j], b_send.at[j])
         if j:
             second_drain(j - 1)
         second_wait(j)
@@ -438,20 +477,19 @@
                 total += got2[j, half, d].astype(F32)
             total = total.astype(BF16)
             for h in range(2):
-                last[pl.ds(h * HF + j * CR, CR), columns[half]] = total[h]
-        for h in range(2):
-            out_copy(j, h).start()
-
-    stage0(0)
-    stage0(1)
-    stage1(0)
-    for j in range(2, CH):
-        stage0(j)
-        stage1(j - 1)
-        stage2(j - 2)
-    stage1(CH - 1)
-    stage2(CH - 2)
-    stage2(CH - 1)
+                diag[0, pl.ds(h * HF + j * CR, CR), columns[half]] = total[h]
+
+    for j in range(CH + 3):
+        if j < CH:
+            stage0(j)
+        if j == X_AT:
+            x_start()
+        if 1 <= j <= CH:
+            stage_hop(j - 1)
+        if 2 <= j <= CH + 1:
+            stage1(j - 2)
+        if j >= 3:
+            stage2(j - 3)
 
     def x_wait():
         wait(cross, x_recv)
@@ -467,8 +505,6 @@
     @pl.when(r == back)
     def _():
         wait(x_relay, xr_send)
-
-    wait(diag, f_sem)
 
 
 def per_device(stiffness, coupling, slave_diag, slave_masters):
@@ -479,28 +515,31 @@
     return pl.pallas_call(
         kernel,
         out_shape=(pltpu.VMEM((NB, QF, FW), BF16), pltpu.VMEM((1, QF, FW), BF16)),
-        in_specs=[any_space, any_space, vmem, vmem],
+        in_specs=[any_space] * 4,
         out_specs=(vmem, vmem),
         scratch_shapes=[
             pltpu.VMEM((2, NS, NS), BF16),
             pltpu.VMEM((2, 2 * FW, NS), BF16),
             pltpu.VMEM((NB, QN, 2, FW), BF16),
+            pltpu.VMEM((NB, QN), F32),
+            pltpu.VMEM((2, NB), jnp.int32),
             pltpu.VMEM((NB, 2 * FW, QN), BF16),
             pltpu.VMEM((2 * FW, QN), BF16),
             pltpu.VMEM((QF, FW), BF16),
             pltpu.VMEM((2, FW, NS), BF16),
             pltpu.VMEM((2, 3, FW, FW), BF16),
             pltpu.VMEM((CH, 2, 4, 4, 2, CR, HC), BF16),
-            pltpu.VMEM((CH, 2, 3, 4, 2, CR, HC), BF16),
+            pltpu.VMEM((CH, 2, 2, 2, 2, CR, HC), BF16),
+            pltpu.VMEM((CH, 2, 2, 4, 2, CR, HC), BF16),
             pltpu.VMEM((CH, 2, 4, 2, CR, HC), BF16),
             pltpu.VMEM((CH, 2, 4, 2, CR, HC), BF16),
-            pltpu.VMEM((QF, FW), BF16),
             pltpu.VMEM((2, 8, 128), jnp.int32),
             pltpu.VMEM((2, 2, 8, 128), jnp.int32),
             pltpu.SMEM((2, 2, 8, 128), jnp.int32),
             dma((2,)), dma((2,)), dma((NB,)), dma((2,)), dma((2, 2)), dma, dma((2,)),
             dma((2, CH)), dma((CH,)), dma((2,)), dma, dma, dma,
-            dma((CH,)), dma((CH,)), dma((CH,)), dma((CH,)), dma, dma((2,)), dma, dma, pltpu.SemaphoreType.REGULAR((2,)),
+            dma((CH,)), dma((CH,)), dma((CH,)), dma((CH,)), dma((CH,)), dma((CH,)), dma((2,)), dma, dma,
+            dma((2,)), pltpu.SemaphoreType.REGULAR((2,)),
             *[pltpu.VMEM((NONE + 1, CR, FW), BF16)] * CH,
         ],
         compiler_params=pltpu.CompilerParams(

time: 139 us -> 137 us (0.986)
    pallas_call x1, Pallas kernels: 136 us -> 135 us  [per_device(): pl.pallas_call(kernel, out_shape=(pltpu.VMEM((NB, QF, FW), BF16), pltpu.V...]
where the time goes in v6:
time: 137 us
  Pallas kernels  135 us (99%)
  local copies, waits for them, and re-layouts  1.83 us (1%)
    pallas_call x1, Pallas kernels, per_device(): pl.pallas_call(kernel, out_shape=(pltpu.VMEM((NB, QF, FW), BF16), pltpu.V...  135 us

profile of v6, /device:TPU:1, one launch (start us, length us, event | category | flops | bytes accessed | tf_op | source)
XLA Modules:
  0.0 137.1 jit_solution(2557077040672905130)
XLA Ops:
  0.6 134.6 %condense.1 = (bf16[5,192,768]{2,1,0:T(8,128)(2,1)S(1)}, bf16[1,192,768]{2,1,0:T(8,128)(2,1)S(1)}) custom-call(bf16[5,256,1024]{2,1,0:T(8,128)(2,1)} %stiff.1, bf16[5,256,2,768]{3,2,1,0:T(2,128)(2,1)} %coup.1, f32[5,256]{1,0:T(8,128)} %scale_in.1, s32[2,5]{1,0:T(2,128)} %bitcast.1), custom_call_target="tpu_custom_call" | custom-call | flops 8556380160 | bytes 9437184 | tf_op jit(solution)/shard_map/condense/pallas_call | solution.py:515
  135.2 1.1 copy.8
  136.4 0.7 copy.9

commit v7 on v6

--- a/solution.py
+++ b/solution.py
@@ -507,12 +507,21 @@
         wait(x_relay, xr_send)
 
 
+def store(cross, diag, cross_out, diag_out, sem):
+    copies = [pltpu.make_async_copy(cross.at[b], cross_out.at[b], sem.at[b]) for b in range(NB)]
+    copies.append(pltpu.make_async_copy(diag, diag_out, sem.at[NB]))
+    for copy in copies:
+        copy.start()
+    for copy in copies:
+        copy.wait()
+
+
 def per_device(stiffness, coupling, slave_diag, slave_masters):
     any_space = pl.BlockSpec(memory_space=pl.ANY)
     vmem = pl.BlockSpec(memory_space=pltpu.VMEM)
     dma = pltpu.SemaphoreType.DMA
     flops = 2 * NB * (2 * NS * NS * FW + 3 * FW * FW * NS) // 4
-    return pl.pallas_call(
+    cross, diag = pl.pallas_call(
         kernel,
         out_shape=(pltpu.VMEM((NB, QF, FW), BF16), pltpu.VMEM((1, QF, FW), BF16)),
         in_specs=[any_space] * 4,
@@ -548,6 +557,20 @@
         cost_estimate=pl.CostEstimate(flops=flops, bytes_accessed=9 * 2**20, transcendentals=0),
         name="condense",
     )(stiffness, coupling, slave_diag, slave_masters.T)
+    cross = pltpu.with_memory_space_constraint(cross, pltpu.VMEM)
+    diag = pltpu.with_memory_space_constraint(diag, pltpu.VMEM)
+    return pl.pallas_call(
+        store,
+        out_shape=(
+            jax.ShapeDtypeStruct((NB, QF, FW), BF16),
+            jax.ShapeDtypeStruct((1, QF, FW), BF16),
+        ),
+        in_specs=[vmem, vmem],
+        out_specs=(any_space, any_space),
+        scratch_shapes=[dma((NB + 1,))],
+        cost_estimate=pl.CostEstimate(flops=0, bytes_accessed=4 * 2**20, transcendentals=0),
+        name="store",
+    )(cross, diag)
 
 
 def solution(mesh):

time: 137 us -> 137 us (level)
  local copies, waits for them, and re-layouts: 1.83 us -> 0 us
    unnamed x2 -> x0, local copies, waits for them, and re-layouts: 1.83 us -> none
where the time goes in v7:
time: 137 us
  Pallas kernels  136 us (99%)
    pallas_call x1, Pallas kernels, per_device(): pl.pallas_call(kernel, out_shape=(pltpu.VMEM((NB, QF, FW), BF16), pltpu.V...  135 us

profile of v7, /device:TPU:1, one launch (start us, length us, event | category | flops | bytes accessed | tf_op | source)
XLA Modules:
  0.0 136.7 jit_solution(16233565141092649415)
XLA Ops:
  0.6 134.6 %condense.1 = (bf16[5,192,768]{2,1,0:T(8,128)(2,1)S(1)}, bf16[1,192,768]{2,1,0:T(8,128)(2,1)S(1)}) custom-call(bf16[5,256,1024]{2,1,0:T(8,128)(2,1)} %stiff.1, bf16[5,256,2,768]{3,2,1,0:T(2,128)(2,1)} %coup.1, f32[5,256]{1,0:T(8,128)} %scale_in.1, s32[2,5]{1,0:T(2,128)} %bitcast.1), custom_call_target="tpu_custom_call" | custom-call | flops 8556380160 | bytes 9437184 | tf_op jit(solution)/shard_map/condense/pallas_call | solution.py:524
  135.2 1.3 store.1

commit v8 on v7

--- a/solution.py
+++ b/solution.py
@@ -21,7 +21,7 @@
 NONE = 4 * NB
 CH = 6
 CR = HF // CH
-X_AT = 4
+X_AT = 3
 
 
 def kernel(
@@ -212,11 +212,9 @@
     def x_forward():
         return remote(x_relay, cross.at[4], xr_send, x_recv, (far, c))
 
-    def x_copies(slot, b):
+    def x_copies(slot, b, places):
         copies = []
-        for dq in range(ROWS):
-            if slot == 0 and dq == 2:
-                continue
+        for dq in places:
             q = lax.rem(r + dq, ROWS)
             src = fills.at[slot, 2, pl.ds(pl.multiple_of(q * QF, QF), QF)]
             if dq:
@@ -349,13 +347,16 @@
         for stage in range(2):
             pl.semaphore_wait(ready.at[stage], 1)
 
+    for copy in x_copies(1, r, (2,)):
+        copy.start()
+
     def x_start():
-        for copy in x_copies(1, r):
+        for copy in x_copies(1, r, (0, 1, 3)):
             copy.start()
 
         @pl.when(owner)
         def _():
-            for copy in x_copies(0, 4):
+            for copy in x_copies(0, 4, (0, 1, 3)):
                 copy.start()
 
         @pl.when(r == back)

time: 137 us -> 138 us (level)
  the two profiles are of different devices: /device:TPU:1 before, /device:TPU:7 now
where the time goes in v8:
time: 138 us
  Pallas kernels  138 us (100%)
    pallas_call x1, Pallas kernels, per_device(): pl.pallas_call(kernel, out_shape=(pltpu.VMEM((NB, QF, FW), BF16), pltpu.V...  136 us

profile of v8, /device:TPU:7, one launch (start us, length us, event | category | flops | bytes accessed | tf_op | source)
XLA Modules:
  0.0 138.4 jit_solution(13352406674747938426)
XLA Ops:
  0.6 136.3 %condense.1 = (bf16[5,192,768]{2,1,0:T(8,128)(2,1)S(1)}, bf16[1,192,768]{2,1,0:T(8,128)(2,1)S(1)}) custom-call(bf16[5,256,1024]{2,1,0:T(8,128)(2,1)} %stiff.1, bf16[5,256,2,768]{3,2,1,0:T(2,128)(2,1)} %coup.1, f32[5,256]{1,0:T(8,128)} %scale_in.1, s32[2,5]{1,0:T(2,128)} %bitcast.1), custom_call_target="tpu_custom_call" | custom-call | flops 8556380160 | bytes 9437184 | tf_op jit(solution)/shard_map/condense/pallas_call | solution.py:525
  136.9 1.3 store.1

commit v9 on v7

--- a/solution.py
+++ b/solution.py
@@ -508,8 +508,12 @@
 
 
 def store(cross, diag, cross_out, diag_out, sem):
-    copies = [pltpu.make_async_copy(cross.at[b], cross_out.at[b], sem.at[b]) for b in range(NB)]
-    copies.append(pltpu.make_async_copy(diag, diag_out, sem.at[NB]))
+    copies = []
+    for h in range(2):
+        rows = pl.ds(h * HF, HF)
+        for b in range(NB):
+            copies.append(pltpu.make_async_copy(cross.at[b, rows], cross_out.at[b, rows], sem.at[h, b]))
+        copies.append(pltpu.make_async_copy(diag.at[0, rows], diag_out.at[0, rows], sem.at[h, NB]))
     for copy in copies:
         copy.start()
     for copy in copies:
@@ -567,7 +571,7 @@
         ),
         in_specs=[vmem, vmem],
         out_specs=(any_space, any_space),
-        scratch_shapes=[dma((NB + 1,))],
+        scratch_shapes=[dma((2, NB + 1))],
         cost_estimate=pl.CostEstimate(flops=0, bytes_accessed=4 * 2**20, transcendentals=0),
         name="store",
     )(cross, diag)

time: 137 us -> 137 us (level)
  no operation moved by 1% of the time
where the time goes in v9:
time: 137 us
  Pallas kernels  136 us (99%)
    pallas_call x1, Pallas kernels, per_device(): pl.pallas_call(kernel, out_shape=(pltpu.VMEM((NB, QF, FW), BF16), pltpu.V...  135 us

profile of v9, /device:TPU:1, one launch (start us, length us, event | category | flops | bytes accessed | tf_op | source)
XLA Modules:
  0.0 136.7 jit_solution(14692174494828505969)
XLA Ops:
  0.6 134.6 %condense.1 = (bf16[5,192,768]{2,1,0:T(8,128)(2,1)S(1)}, bf16[1,192,768]{2,1,0:T(8,128)(2,1)S(1)}) custom-call(bf16[5,256,1024]{2,1,0:T(8,128)(2,1)} %stiff.1, bf16[5,256,2,768]{3,2,1,0:T(2,128)(2,1)} %coup.1, f32[5,256]{1,0:T(8,128)} %scale_in.1, s32[2,5]{1,0:T(2,128)} %bitcast.1), custom_call_target="tpu_custom_call" | custom-call | flops 8556380160 | bytes 9437184 | tf_op jit(solution)/shard_map/condense/pallas_call | solution.py:528
  135.2 1.3 store.1
